TPU v7x, 32 devices: a whole 2x2x4 slice. The times are simulated.
32 devices in a mesh: pipe: 2 (over core), tensor: 4 (over z), dp: 4 (over y, x).
Axes of the slice: x: 2, y: 2, z: 4, core: 2. Of those that a mesh axis runs over, the one named last changes fastest.
Arguments:
- features: float32 [16, 448, 768], P('dp', 'tensor'), may hold values from -6 to 6
- cotangent: float32 [16, 448, 768], P('dp', 'tensor'), may hold values from -6 to 6
- norm_gains: float32 [2, 2, 768], P('pipe'), may hold values from 0.1 to 1.9
- norm_shifts: float32 [2, 2, 768], P('pipe'), may hold values from -1.75 to 1.75
- qkv_weight: bfloat16 [2, 768, 12, 192], P('pipe', None, 'tensor'), may hold values from -0.21875 to 0.21875
- qv_bias: float32 [2, 2, 12, 64], P('pipe', None, 'tensor'), may hold values from -1.75 to 1.75
- out_weight: bfloat16 [2, 12, 64, 768], P('pipe', 'tensor'), may hold values from -1.25 to 1.25
- out_bias: float32 [2, 2, 768], P('pipe'), may hold values from -1.75 to 1.75
- up_weight: bfloat16 [2, 768, 3072], P('pipe', None, 'tensor'), may hold values from -0.21875 to 0.21875
- up_bias: float32 [2, 3072], P('pipe', 'tensor'), may hold values from -1.75 to 1.75
- down_weight: bfloat16 [2, 3072, 768], P('pipe', 'tensor'), may hold values from -0.109375 to 0.109375
Outputs:
- boundary: float32 [2, 16, 448, 768], P('pipe', 'dp', 'tensor')
- gain_grads: float32 [2, 2, 768], P('pipe')
- shift_grads: float32 [2, 2, 768], P('pipe')
- qkv_grads: float32 [2, 768, 12, 192], P('pipe', None, 'tensor')
- qv_bias_grads: float32 [2, 2, 12, 64], P('pipe', None, 'tensor')
- out_grads: float32 [2, 12, 64, 768], P('pipe', 'tensor')
- out_bias_grads: float32 [2, 2, 768], P('pipe')
- up_grads: float32 [2, 768, 3072], P('pipe', None, 'tensor')
- up_bias_grads: float32 [2, 3072], P('pipe', 'tensor')
- down_grads: float32 [2, 3072, 768], P('pipe', 'tensor')
All inputs are finite; a program needn't handle non-finite values.
Results may differ from a plain program's by a relative error of at most 0.018.
Values may be sent and summed in bfloat16 or wider, within the bound.
A program may use at most 192 MiB of HBM per device.

v0:
```python
import jax
import jax.numpy as jnp
from jax import lax
from jax.sharding import PartitionSpec as P

MICRO = 4
MB_CLIPS = 1


EPSILON = 1e-05


def from_behind(block, axis, distance):
    devices = range(lax.axis_size(axis))
    route = [(i - distance, i) for i in devices if i - distance in devices]
    return lax.ppermute(block, axis, route)


def norm_rows(values, gain_row, shift_row):
    row_mean = jnp.mean(values, axis=-1, keepdims=True)
    centered = values - row_mean
    variance = jnp.mean(centered * centered, axis=-1, keepdims=True)
    return centered * lax.rsqrt(variance + EPSILON) * gain_row + shift_row


def softmax_rows(scores):
    row_peak = jnp.max(scores, axis=-1, keepdims=True)
    powers = jnp.exp(scores - row_peak)
    return powers / jnp.sum(powers, axis=-1, keepdims=True)


def exact_gelu(values):
    return jax.nn.gelu(values, approximate=False)


def gather_normed(share_rows, gain_row, shift_row):
    normed = norm_rows(share_rows, gain_row, shift_row).astype(jnp.bfloat16)
    return lax.all_gather(normed, "tensor", axis=1, tiled=True)


def sum_branch(pieces):
    return lax.psum_scatter(
        pieces.astype(jnp.bfloat16), "tensor", scatter_dimension=1, tiled=True
    ).astype(jnp.float32)


def gather_grads(grad_rows):
    return lax.all_gather(grad_rows.astype(jnp.bfloat16), "tensor", axis=1, tiled=True)


def sum_normed_grads(pieces):
    return lax.psum_scatter(
        pieces.astype(jnp.bfloat16), "tensor", scatter_dimension=1, tiled=True
    ).astype(jnp.float32)


def store_slot(buffer, item_rows, slot_index, is_valid):
    updated = lax.dynamic_update_index_in_dim(buffer, item_rows, slot_index, 0)
    return jnp.where(is_valid, updated, buffer)


def read_slot(buffer, slot_index):
    return lax.dynamic_index_in_dim(buffer, slot_index, 0, keepdims=False)


def add_valid(totals, parts, is_valid):
    return tuple(
        (jnp.where(is_valid, running + piece, running) for running, piece in zip(totals, parts))
    )


def per_device(
    features,
    cotangent,
    norm_gains,
    norm_shifts,
    qkv_weight,
    qv_bias,
    out_weight,
    out_bias,
    up_weight,
    up_bias,
    down_weight,
):
    section_index = lax.axis_index("pipe")
    leading = section_index == 0
    model_width = features.shape[2]
    seq_share = features.shape[1]
    full_length = seq_share * lax.axis_size("tensor")
    heads_here = qkv_weight.shape[2]
    head_dim = qv_bias.shape[3]
    hidden_here = up_weight.shape[2]
    score_scale = head_dim ** (-0.5)
    norm_gain = norm_gains[0]
    norm_shift = norm_shifts[0]
    qkv_flat = qkv_weight[0].reshape(model_width, heads_here * 3 * head_dim)
    bias_pair = qv_bias[0]
    out_flat = out_weight[0].reshape(heads_here * head_dim, model_width)
    end_bias = out_bias[0]
    up_matrix = up_weight[0]
    up_vector = up_bias[0]
    down_matrix = down_weight[0]
    f32 = jnp.float32
    bf16 = jnp.bfloat16

    def attend(gathered):
        clip_count = gathered.shape[0]
        projected = jnp.dot(gathered.reshape(-1, model_width), qkv_flat, preferred_element_type=f32)
        projected = projected.reshape(clip_count, full_length, heads_here, 3 * head_dim)
        queries = (projected[..., :head_dim] + bias_pair[0]).astype(bf16)
        key_rows = projected[..., head_dim : 2 * head_dim].astype(bf16)
        values = (projected[..., 2 * head_dim :] + bias_pair[1]).astype(bf16)
        scores = (
            jnp.einsum("bqhe,bkhe->bhqk", queries, key_rows, preferred_element_type=f32)
            * score_scale
        )
        probability = softmax_rows(scores)
        probability_low = probability.astype(bf16)
        attended = jnp.einsum(
            "bhqk,bkhe->bqhe", probability_low, values, preferred_element_type=f32
        ).astype(bf16)
        return (queries, key_rows, values, probability, probability_low, attended)

    micro_inputs = features.reshape(MICRO, MB_CLIPS, seq_share, model_width)
    micro_grads = cotangent.reshape(MICRO, MB_CLIPS, seq_share, model_width)
    share_zeros = jnp.zeros((MB_CLIPS, seq_share, model_width), f32)
    kept_entries = jnp.zeros((MICRO, MB_CLIPS, seq_share, model_width), f32)
    kept_middles = jnp.zeros((MICRO, MB_CLIPS, seq_share, model_width), f32)
    block_outputs = jnp.zeros((MICRO, MB_CLIPS, seq_share, model_width), f32)
    mlp_totals = (
        jnp.zeros((model_width, hidden_here), f32),
        jnp.zeros((hidden_here,), f32),
        jnp.zeros((hidden_here, model_width), f32),
    )
    attention_totals = (
        jnp.zeros((model_width, heads_here * 3 * head_dim), f32),
        jnp.zeros((2, heads_here, head_dim), f32),
        jnp.zeros((heads_here * head_dim, model_width), f32),
    )
    shared_totals = tuple((jnp.zeros((model_width,), f32) for position_name in range(6)))
    input_grads = jnp.zeros((MICRO, MB_CLIPS, seq_share, model_width), f32)
    arrived = share_zeros
    returned = share_zeros
    for moment in range(MICRO + 2):
        ahead = moment - section_index
        ahead_valid = (ahead >= 0) & (ahead < MICRO)
        ahead_slot = jnp.clip(ahead, 0, MICRO - 1)
        entry_rows = jnp.where(leading, micro_inputs[min(moment, MICRO - 1)], arrived)
        forward_gathered = gather_normed(entry_rows, norm_gain[0], norm_shift[0])
        forward_attended = attend(forward_gathered)[5]
        pieces = jnp.dot(
            forward_attended.reshape(-1, heads_here * head_dim),
            out_flat,
            preferred_element_type=f32,
        )
        forward_middle = (
            entry_rows + sum_branch(pieces.reshape(forward_gathered.shape)) + end_bias[0]
        )
        forward_gathered_two = gather_normed(forward_middle, norm_gain[1], norm_shift[1])
        forward_hidden_pre = (
            jnp.dot(
                forward_gathered_two.reshape(-1, model_width), up_matrix, preferred_element_type=f32
            )
            + up_vector
        )
        forward_active = exact_gelu(forward_hidden_pre).astype(bf16)
        pieces_two = jnp.dot(forward_active, down_matrix, preferred_element_type=f32).reshape(
            forward_gathered.shape
        )
        result = forward_middle + sum_branch(pieces_two) + end_bias[1]
        result, middle, gathered, gathered_two = (
            result,
            forward_middle,
            forward_gathered,
            forward_gathered_two,
        )
        kept_entries = store_slot(kept_entries, entry_rows, ahead_slot, ahead_valid)
        kept_middles = store_slot(kept_middles, middle, ahead_slot, ahead_valid)
        block_outputs = store_slot(block_outputs, result, ahead_slot, ahead_valid)
        if moment < MICRO:
            arrived = from_behind(result.astype(jnp.bfloat16), "pipe", 1).astype(result.dtype)
        behind = moment - 2 + section_index
        behind_valid = (behind >= 0) & (behind < MICRO)
        behind_slot = jnp.clip(behind, 0, MICRO - 1)
        incoming = jnp.where(leading, returned, micro_grads[min(max(moment - 1, 0), MICRO - 1)])
        back_entry = read_slot(kept_entries, behind_slot)
        back_middle = read_slot(kept_middles, behind_slot)
        back_gathered = gather_normed(back_entry, norm_gain[0], norm_shift[0])
        back_gathered_two = gather_normed(back_middle, norm_gain[1], norm_shift[1])
        backward_rows_grad = gather_grads(incoming)
        flat_two = back_gathered_two.reshape(-1, model_width)
        hidden_pre = jnp.dot(flat_two, up_matrix, preferred_element_type=f32) + up_vector
        active, gelu_pull = jax.vjp(exact_gelu, hidden_pre)
        active_low = active.astype(bf16)
        backward_flat_grad = backward_rows_grad.reshape(-1, model_width)
        down_grad = jnp.einsum(
            "nf,nd->fd", active_low, backward_flat_grad, preferred_element_type=f32
        )
        active_grad = jnp.einsum(
            "nd,fd->nf", backward_flat_grad, down_matrix, preferred_element_type=f32
        )
        pre_grad = gelu_pull(active_grad)[0].astype(bf16)
        up_bias_grad = jnp.sum(pre_grad.astype(f32), axis=0)
        up_grad = jnp.einsum("nd,nf->df", flat_two, pre_grad, preferred_element_type=f32)
        backward_normed_pieces = jnp.einsum(
            "nf,df->nd", pre_grad, up_matrix, preferred_element_type=f32
        )
        backward_normed_grad = sum_normed_grads(
            backward_normed_pieces.reshape(backward_rows_grad.shape)
        )
        backward_norm_pull = jax.vjp(norm_rows, back_middle, norm_gain[1], norm_shift[1])[1]
        backward_middle_grad, backward_gain_grad, backward_shift_grad = backward_norm_pull(
            backward_normed_grad
        )
        backward_middle_grad = backward_middle_grad + incoming
        backward_shared = (backward_gain_grad, backward_shift_grad, jnp.sum(incoming, axis=(0, 1)))
        mlp_parts = (up_grad, up_bias_grad, down_grad)
        mlp_totals = add_valid(mlp_totals, mlp_parts, behind_valid)
        rows_grad = gather_grads(backward_middle_grad)
        (
            backward_queries,
            backward_key_rows,
            backward_values,
            backward_probability,
            backward_probability_low,
            backward_attended,
        ) = attend(back_gathered)
        flat_grad = rows_grad.reshape(-1, model_width)
        out_grad = jnp.einsum(
            "nc,nd->cd",
            backward_attended.reshape(-1, heads_here * head_dim),
            flat_grad,
            preferred_element_type=f32,
        )
        attended_grad = jnp.einsum(
            "nd,cd->nc", flat_grad, out_flat, preferred_element_type=f32
        ).astype(bf16)
        attended_grad = attended_grad.reshape(backward_attended.shape)
        probability_grad = jnp.einsum(
            "bqhe,bkhe->bhqk", attended_grad, backward_values, preferred_element_type=f32
        )
        values_grad = jnp.einsum(
            "bhqk,bqhe->bkhe", backward_probability_low, attended_grad, preferred_element_type=f32
        ).astype(bf16)
        row_inner = jnp.sum(backward_probability * probability_grad, axis=-1, keepdims=True)
        scores_grad = (backward_probability * (probability_grad - row_inner)).astype(bf16)
        queries_grad = (
            jnp.einsum(
                "bhqk,bkhe->bqhe", scores_grad, backward_key_rows, preferred_element_type=f32
            )
            * score_scale
        ).astype(bf16)
        keys_grad = (
            jnp.einsum("bhqk,bqhe->bkhe", scores_grad, backward_queries, preferred_element_type=f32)
            * score_scale
        ).astype(bf16)
        projected_grad = jnp.concatenate([queries_grad, keys_grad, values_grad], axis=-1)
        bias_grad = jnp.stack(
            [
                jnp.sum(queries_grad.astype(f32), axis=(0, 1)),
                jnp.sum(values_grad.astype(f32), axis=(0, 1)),
            ]
        )
        flat_projected = projected_grad.reshape(-1, heads_here * 3 * head_dim)
        qkv_grad = jnp.einsum(
            "nd,nc->dc",
            back_gathered.reshape(-1, model_width),
            flat_projected,
            preferred_element_type=f32,
        )
        normed_pieces = jnp.einsum(
            "nc,dc->nd", flat_projected, qkv_flat, preferred_element_type=f32
        )
        normed_grad = sum_normed_grads(normed_pieces.reshape(rows_grad.shape))
        norm_pull = jax.vjp(norm_rows, back_entry, norm_gain[0], norm_shift[0])[1]
        entry_grad, gain_grad, shift_grad = norm_pull(normed_grad)
        entry_grad = entry_grad + backward_middle_grad
        shared = (gain_grad, shift_grad, jnp.sum(backward_middle_grad, axis=(0, 1)))
        entry_grad, attention_parts, shared_one = (
            entry_grad,
            (qkv_grad, bias_grad, out_grad),
            shared,
        )
        attention_totals = add_valid(attention_totals, attention_parts, behind_valid)
        shared_totals = add_valid(shared_totals, shared_one + backward_shared, behind_valid)
        input_grads = store_slot(input_grads, entry_grad, behind_slot, behind_valid)
        if 1 <= moment <= MICRO:
            returned = from_behind(entry_grad.astype(jnp.bfloat16), "pipe", -1).astype(
                entry_grad.dtype
            )
    summed = (
        lax.psum(mlp_totals[0].astype(jnp.bfloat16), "dp").astype(jnp.float32),
        lax.psum(mlp_totals[1].astype(jnp.bfloat16), "dp").astype(jnp.float32),
        lax.psum(mlp_totals[2].astype(jnp.bfloat16), "dp").astype(jnp.float32),
        lax.psum(attention_totals[0].astype(jnp.bfloat16), "dp").astype(jnp.float32),
        lax.psum(attention_totals[1].astype(jnp.bfloat16), "dp").astype(jnp.float32),
        lax.psum(attention_totals[2].astype(jnp.bfloat16), "dp").astype(jnp.float32),
    )
    mlp_totals = (summed[0], summed[1], summed[2])
    attention_totals = (summed[3], summed[4], summed[5])
    gain_stack = jnp.stack([shared_totals[0], shared_totals[3]])
    shift_stack = jnp.stack([shared_totals[1], shared_totals[4]])
    bias_stack = jnp.stack([shared_totals[2], shared_totals[5]])
    gain_sum, shift_sum, bias_sum = lax.psum(
        (gain_stack, shift_stack, bias_stack), ("tensor", "dp")
    )
    boundary = jnp.where(leading, input_grads, block_outputs).reshape(
        1, MICRO * MB_CLIPS, seq_share, model_width
    )
    return (
        boundary,
        gain_sum.reshape(1, 2, model_width),
        shift_sum.reshape(1, 2, model_width),
        attention_totals[0].reshape(1, model_width, heads_here, 3 * head_dim),
        attention_totals[1].reshape(1, 2, heads_here, head_dim),
        attention_totals[2].reshape(1, heads_here, head_dim, model_width),
        bias_sum.reshape(1, 2, model_width),
        mlp_totals[0].reshape(1, model_width, hidden_here),
        mlp_totals[1].reshape(1, hidden_here),
        mlp_totals[2].reshape(1, hidden_here, model_width),
    )


def solution(mesh):
    in_specs = (
        P("dp", "tensor", None),
        P("dp", "tensor", None),
        P("pipe", None, None),
        P("pipe", None, None),
        P("pipe", None, "tensor", None),
        P("pipe", None, "tensor", None),
        P("pipe", "tensor", None, None),
        P("pipe", None, None),
        P("pipe", None, "tensor"),
        P("pipe", "tensor"),
        P("pipe", "tensor", None),
    )
    out_specs = (
        P("pipe", "dp", "tensor", None),
        P("pipe", None, None),
        P("pipe", None, None),
        P("pipe", None, "tensor", None),
        P("pipe", None, "tensor", None),
        P("pipe", "tensor", None, None),
        P("pipe", None, None),
        P("pipe", None, "tensor"),
        P("pipe", "tensor"),
        P("pipe", "tensor", None),
    )
    return jax.shard_map(
        per_device, mesh=mesh, in_specs=in_specs, out_specs=out_specs, check_vma=False
    )
```

profile of v0, /device:TPU:0, one launch (start us, length us, event | category | flops | bytes accessed | tf_op | source)
XLA Modules:
  0.0 1415.3 jit_solution(12174155388877003567)
XLA Ops:
  11.7 20.2 %all_gather.103 = bf16[1,448,768]{2,1,0:T(8,128)(2,1)S(1)} all-gather(bf16[1,112,768]{2,1,0:T(8,128)(2,1)S(1)} %add_convert_fusion.26), channel_id=1, replica_groups=mesh['pipe'=2,'tensor'=4,'dp'=4] {'tensor'}, dimensions={1}, use_global_device_ids=true | all-gather | bytes 860160 | tf_op jit(solution)/shard_map/all_gather | solution.py:38
  41.2 22.4 %reduce-scatter.23.cloned.1.call-done = bf16[1,112,768]{2,1,0:T(8,128)(2,1)} async-done(((bf16[1,448,768]{2,1,0:T(8,128)(2,1)}), bf16[1,112,768]{2,1,0:T(8,128)(2,1)}) %reduce-scatter.23.cloned.1.call-update) | async-done | bytes 172048 | tf_op jit(solution)/shard_map/reduce_scatter | solution.py:42
  65.1 17.2 %all_gather.107 = bf16[1,448,768]{2,1,0:T(8,128)(2,1)} all-gather(bf16[1,112,768]{2,1,0:T(8,128)(2,1)S(1)} %add_convert_fusion.24), channel_id=1, replica_groups=mesh['pipe'=2,'tensor'=4,'dp'=4] {'tensor'}, dimensions={1}, use_global_device_ids=true | all-gather | bytes 860160 | tf_op jit(solution)/shard_map/all_gather | solution.py:38
  82.2 6.5 fusion.174
  88.9 22.7 %reduce-scatter.29.cloned.1.call-done = bf16[1,112,768]{2,1,0:T(8,128)(2,1)} async-done(((bf16[1,448,768]{2,1,0:T(8,128)(2,1)}), bf16[1,112,768]{2,1,0:T(8,128)(2,1)}) %reduce-scatter.29.cloned.1.call-update) | async-done | bytes 172048 | tf_op jit(solution)/shard_map/reduce_scatter | solution.py:42
  120.1 17.0 %all_gather.109 = bf16[1,448,768]{2,1,0:T(8,128)(2,1)S(1)} all-gather(bf16[1,112,768]{2,1,0:T(8,128)(2,1)S(1)} %add_convert_fusion.22), channel_id=1, replica_groups=mesh['pipe'=2,'tensor'=4,'dp'=4] {'tensor'}, dimensions={1}, use_global_device_ids=true | all-gather | bytes 860160 | tf_op jit(solution)/shard_map/all_gather | solution.py:38
  138.8 4.3 fusion.1063
  146.8 21.5 %reduce-scatter.31.cloned.1.call-done = bf16[1,112,768]{2,1,0:T(8,128)(2,1)} async-done(((bf16[1,448,768]{2,1,0:T(8,128)(2,1)}), bf16[1,112,768]{2,1,0:T(8,128)(2,1)}) %reduce-scatter.31.cloned.1.call-update) | async-done | bytes 172048 | tf_op jit(solution)/shard_map/reduce_scatter | solution.py:42
  169.8 17.5 %all_gather.112 = bf16[1,448,768]{2,1,0:T(8,128)(2,1)} all-gather(bf16[1,112,768]{2,1,0:T(8,128)(2,1)S(1)} %add_convert_fusion.20), channel_id=1, replica_groups=mesh['pipe'=2,'tensor'=4,'dp'=4] {'tensor'}, dimensions={1}, use_global_device_ids=true | all-gather | bytes 860160 | tf_op jit(solution)/shard_map/all_gather | solution.py:38
  187.4 6.5 fusion.176
  194.0 22.8 %reduce-scatter.37.cloned.1.call-done = bf16[1,112,768]{2,1,0:T(8,128)(2,1)} async-done(((bf16[1,448,768]{2,1,0:T(8,128)(2,1)}), bf16[1,112,768]{2,1,0:T(8,128)(2,1)}) %reduce-scatter.37.cloned.1.call-update) | async-done | bytes 172048 | tf_op jit(solution)/shard_map/reduce_scatter | solution.py:42
  224.6 17.2 %all_gather.114 = bf16[1,448,768]{2,1,0:T(8,128)(2,1)S(1)} all-gather(bf16[1,112,768]{2,1,0:T(8,128)(2,1)S(1)} %add_convert_fusion.18), channel_id=1, replica_groups=mesh['pipe'=2,'tensor'=4,'dp'=4] {'tensor'}, dimensions={1}, use_global_device_ids=true | all-gather | bytes 860160 | tf_op jit(solution)/shard_map/all_gather | solution.py:38
  252.0 21.8 %reduce-scatter.39.cloned.1.call-done = bf16[1,112,768]{2,1,0:T(8,128)(2,1)} async-done(((bf16[1,448,768]{2,1,0:T(8,128)(2,1)}), bf16[1,112,768]{2,1,0:T(8,128)(2,1)}) %reduce-scatter.39.cloned.1.call-update) | async-done | bytes 172048 | tf_op jit(solution)/shard_map/reduce_scatter | solution.py:42
  275.8 16.8 %all_gather.118 = bf16[1,448,768]{2,1,0:T(8,128)(2,1)S(1)} all-gather(bf16[1,112,768]{2,1,0:T(8,128)(2,1)S(1)} %add_convert_fusion.16), channel_id=1, replica_groups=mesh['pipe'=2,'tensor'=4,'dp'=4] {'tensor'}, dimensions={1}, use_global_device_ids=true | all-gather | bytes 860160 | tf_op jit(solution)/shard_map/all_gather | solution.py:38
  292.6 6.3 fusion.178
  300.0 22.9 %all_gather.105 = bf16[1,448,768]{2,1,0:T(8,128)(2,1)} all-gather(bf16[1,112,768]{2,1,0:T(8,128)(2,1)S(1)} %fusion.671), channel_id=1, replica_groups=mesh['pipe'=2,'tensor'=4,'dp'=4] {'tensor'}, dimensions={1}, use_global_device_ids=true | all-gather | bytes 860160 | tf_op jit(solution)/shard_map/all_gather | solution.py:48
  337.3 17.5 %all_gather.120 = bf16[1,448,768]{2,1,0:T(8,128)(2,1)S(1)} all-gather(bf16[1,112,768]{2,1,0:T(8,128)(2,1)S(1)} %add_convert_fusion.14), channel_id=1, replica_groups=mesh['pipe'=2,'tensor'=4,'dp'=4] {'tensor'}, dimensions={1}, use_global_device_ids=true | all-gather | bytes 860160 | tf_op jit(solution)/shard_map/all_gather | solution.py:38
  356.5 4.3 fusion.1081
  371.1 15.3 %reduce-scatter.47.cloned.1.call-done = bf16[1,112,768]{2,1,0:T(8,128)(2,1)} async-done(((bf16[1,448,768]{2,1,0:T(8,128)(2,1)}), bf16[1,112,768]{2,1,0:T(8,128)(2,1)}) %reduce-scatter.47.cloned.1.call-update) | async-done | bytes 172048 | tf_op jit(solution)/shard_map/reduce_scatter | solution.py:42
  387.9 17.1 %all_gather.124 = bf16[1,448,768]{2,1,0:T(8,128)(2,1)} all-gather(bf16[1,112,768]{2,1,0:T(8,128)(2,1)S(1)} %add_convert_fusion.12), channel_id=1, replica_groups=mesh['pipe'=2,'tensor'=4,'dp'=4] {'tensor'}, dimensions={1}, use_global_device_ids=true | all-gather | bytes 860160 | tf_op jit(solution)/shard_map/all_gather | solution.py:38
  405.0 6.6 fusion.180
  421.8 12.6 reduce-scatter.53.cloned.1.call-done
  450.2 16.8 %all_gather.130 = bf16[1,448,768]{2,1,0:T(8,128)(2,1)S(1)} all-gather(bf16[1,112,768]{2,1,0:T(8,128)(2,1)S(1)} %get-tuple-element.149), channel_id=1, replica_groups=mesh['pipe'=2,'tensor'=4,'dp'=4] {'tensor'}, dimensions={1}, use_global_device_ids=true | all-gather | bytes 860160 | tf_op jit(solution)/shard_map/all_gather | solution.py:38
  468.7 17.7 %all_gather.119 = bf16[1,448,768]{2,1,0:T(8,128)(2,1)} all-gather(bf16[1,112,768]{2,1,0:T(8,128)(2,1)S(1)} %get-tuple-element.152), channel_id=1, replica_groups=mesh['pipe'=2,'tensor'=4,'dp'=4] {'tensor'}, dimensions={1}, use_global_device_ids=true | all-gather | bytes 860160 | tf_op jit(solution)/shard_map/all_gather | solution.py:38
  490.6 15.6 %all_gather.126 = bf16[1,448,768]{2,1,0:T(8,128)(2,1)S(1)} all-gather(bf16[1,112,768]{2,1,0:T(8,128)(2,1)S(1)} %get-tuple-element.157), channel_id=1, replica_groups=mesh['pipe'=2,'tensor'=4,'dp'=4] {'tensor'}, dimensions={1}, use_global_device_ids=true | all-gather | bytes 860160 | tf_op jit(solution)/shard_map/all_gather | solution.py:38
  518.5 24.7 %all_gather.113 = bf16[1,448,768]{2,1,0:T(8,128)(2,1)S(1)} all-gather(bf16[1,112,768]{2,1,0:T(8,128)(2,1)S(1)} %copy-done.170), channel_id=1, replica_groups=mesh['pipe'=2,'tensor'=4,'dp'=4] {'tensor'}, dimensions={1}, use_global_device_ids=true | all-gather | bytes 860160 | tf_op jit(solution)/shard_map/all_gather | solution.py:38
  544.9 16.2 %all_gather.108 = bf16[1,448,768]{2,1,0:T(8,128)(2,1)S(1)} all-gather(bf16[1,112,768]{2,1,0:T(8,128)(2,1)S(1)} %copy-done.169), channel_id=1, replica_groups=mesh['pipe'=2,'tensor'=4,'dp'=4] {'tensor'}, dimensions={1}, use_global_device_ids=true | all-gather | bytes 860160 | tf_op jit(solution)/shard_map/all_gather | solution.py:38
  562.7 18.2 %all_gather.125 = bf16[1,448,768]{2,1,0:T(8,128)(2,1)} all-gather(bf16[1,112,768]{2,1,0:T(8,128)(2,1)S(1)} %get-tuple-element.156), channel_id=1, replica_groups=mesh['pipe'=2,'tensor'=4,'dp'=4] {'tensor'}, dimensions={1}, use_global_device_ids=true | all-gather | bytes 860160 | tf_op jit(solution)/shard_map/all_gather | solution.py:38
  584.4 18.1 %all_gather.134 = bf16[1,448,768]{2,1,0:T(8,128)(2,1)} all-gather(bf16[1,112,768]{2,1,0:T(8,128)(2,1)S(1)} %get-tuple-element.145), channel_id=1, replica_groups=mesh['pipe'=2,'tensor'=4,'dp'=4] {'tensor'}, dimensions={1}, use_global_device_ids=true | all-gather | bytes 860160 | tf_op jit(solution)/shard_map/all_gather | solution.py:38
  602.5 6.5 fusion.183
  609.1 20.4 %all_gather.104 = bf16[1,448,768]{2,1,0:T(8,128)(2,1)S(1)} all-gather(bf16[1,112,768]{2,1,0:T(8,128)(2,1)S(1)} %get-tuple-element.148), channel_id=1, replica_groups=mesh['pipe'=2,'tensor'=4,'dp'=4] {'tensor'}, dimensions={1}, use_global_device_ids=true | all-gather | bytes 860160 | tf_op jit(solution)/shard_map/all_gather | solution.py:38
  631.0 16.9 %all_gather.110 = bf16[1,448,768]{2,1,0:T(8,128)(2,1)S(1)} all-gather(bf16[1,112,768]{2,1,0:T(8,128)(2,1)S(1)} %get-tuple-element.146), channel_id=1, replica_groups=mesh['pipe'=2,'tensor'=4,'dp'=4] {'tensor'}, dimensions={1}, use_global_device_ids=true | all-gather | bytes 860160 | tf_op jit(solution)/shard_map/all_gather | solution.py:38
  650.2 8.8 convert_reduce_fusion.4
  663.7 20.8 %all_gather.102 = bf16[1,448,768]{2,1,0:T(8,128)(2,1)S(1)} all-gather(bf16[1,112,768]{2,1,0:T(8,128)(2,1)S(1)} %copy-done.161), channel_id=1, replica_groups=mesh['pipe'=2,'tensor'=4,'dp'=4] {'tensor'}, dimensions={1}, use_global_device_ids=true | all-gather | bytes 860160 | tf_op jit(solution)/shard_map/all_gather | solution.py:38
  705.1 16.6 %reduce-scatter.33.cloned.1.call-done = bf16[1,112,768]{2,1,0:T(8,128)(2,1)} async-done(((bf16[1,448,768]{2,1,0:T(8,128)(2,1)}), bf16[1,112,768]{2,1,0:T(8,128)(2,1)}) %reduce-scatter.33.cloned.1.call-update) | async-done | bytes 172048 | tf_op jit(solution)/shard_map/reduce_scatter | solution.py:52
  729.5 16.8 %all_gather.111 = bf16[1,448,768]{2,1,0:T(8,128)(2,1)S(1)} all-gather(bf16[1,112,768]{2,1,0:T(8,128)(2,1)S(1)} %convert_element_type.1070), channel_id=1, replica_groups=mesh['pipe'=2,'tensor'=4,'dp'=4] {'tensor'}, dimensions={1}, use_global_device_ids=true | all-gather | bytes 860160 | tf_op jit(solution)/shard_map/all_gather | solution.py:48
  753.3 22.8 %all_gather.115 = bf16[1,448,768]{2,1,0:T(8,128)(2,1)} all-gather(bf16[1,112,768]{2,1,0:T(8,128)(2,1)} %get-tuple-element.147), channel_id=1, replica_groups=mesh['pipe'=2,'tensor'=4,'dp'=4] {'tensor'}, dimensions={1}, use_global_device_ids=true | all-gather | bytes 860160 | tf_op jit(solution)/shard_map/all_gather | solution.py:38
  785.2 8.6 fusion.57
  796.2 17.3 %all_gather.116 = bf16[1,448,768]{2,1,0:T(8,128)(2,1)S(1)} all-gather(bf16[1,112,768]{2,1,0:T(8,128)(2,1)S(1)} %fusion.731), channel_id=1, replica_groups=mesh['pipe'=2,'tensor'=4,'dp'=4] {'tensor'}, dimensions={1}, use_global_device_ids=true | all-gather | bytes 860160 | tf_op jit(solution)/shard_map/all_gather | solution.py:48
  817.7 4.3 fusion.1104
  822.0 4.4 fusion.1109
  826.4 4.3 fusion.1114
  833.8 6.2 reduce-scatter.41.cloned.1.call-done
  847.1 16.8 %all_gather.117 = bf16[1,448,768]{2,1,0:T(8,128)(2,1)S(1)} all-gather(bf16[1,112,768]{2,1,0:T(8,128)(2,1)S(1)} %convert_element_type.1114), channel_id=1, replica_groups=mesh['pipe'=2,'tensor'=4,'dp'=4] {'tensor'}, dimensions={1}, use_global_device_ids=true | all-gather | bytes 860160 | tf_op jit(solution)/shard_map/all_gather | solution.py:48
  872.1 4.3 fusion.1119
  881.8 22.7 %all_gather.121 = bf16[1,448,768]{2,1,0:T(8,128)(2,1)} all-gather(bf16[1,112,768]{2,1,0:T(8,128)(2,1)S(1)} %copy-done.168), channel_id=1, replica_groups=mesh['pipe'=2,'tensor'=4,'dp'=4] {'tensor'}, dimensions={1}, use_global_device_ids=true | all-gather | bytes 860160 | tf_op jit(solution)/shard_map/all_gather | solution.py:38
  910.4 8.6 fusion.61
  921.4 17.9 %all_gather.122 = bf16[1,448,768]{2,1,0:T(8,128)(2,1)S(1)} all-gather(bf16[1,112,768]{2,1,0:T(8,128)(2,1)S(1)} %fusion.733), channel_id=1, replica_groups=mesh['pipe'=2,'tensor'=4,'dp'=4] {'tensor'}, dimensions={1}, use_global_device_ids=true | all-gather | bytes 860160 | tf_op jit(solution)/shard_map/all_gather | solution.py:48
  955.3 10.5 reduce-scatter.49.cloned.1.call-done
  973.0 16.8 %all_gather.123 = bf16[1,448,768]{2,1,0:T(8,128)(2,1)S(1)} all-gather(bf16[1,112,768]{2,1,0:T(8,128)(2,1)S(1)} %convert_element_type.1158), channel_id=1, replica_groups=mesh['pipe'=2,'tensor'=4,'dp'=4] {'tensor'}, dimensions={1}, use_global_device_ids=true | all-gather | bytes 860160 | tf_op jit(solution)/shard_map/all_gather | solution.py:48
  1008.7 22.2 %all_gather.127 = bf16[1,448,768]{2,1,0:T(8,128)(2,1)} all-gather(bf16[1,112,768]{2,1,0:T(8,128)(2,1)S(1)} %copy-done.167), channel_id=1, replica_groups=mesh['pipe'=2,'tensor'=4,'dp'=4] {'tensor'}, dimensions={1}, use_global_device_ids=true | all-gather | bytes 860160 | tf_op jit(solution)/shard_map/all_gather | solution.py:38
  1036.9 8.6 fusion.65
  1048.0 17.3 %all_gather.128 = bf16[1,448,768]{2,1,0:T(8,128)(2,1)S(1)} all-gather(bf16[1,112,768]{2,1,0:T(8,128)(2,1)S(1)} %fusion.735), channel_id=1, replica_groups=mesh['pipe'=2,'tensor'=4,'dp'=4] {'tensor'}, dimensions={1}, use_global_device_ids=true | all-gather | bytes 860160 | tf_op jit(solution)/shard_map/all_gather | solution.py:48
  1069.5 22.5 %all_gather.106 = bf16[1,448,768]{2,1,0:T(8,128)(2,1)S(1)} all-gather(bf16[1,112,768]{2,1,0:T(8,128)(2,1)} %convert_element_type.1029), channel_id=1, replica_groups=mesh['pipe'=2,'tensor'=4,'dp'=4] {'tensor'}, dimensions={1}, use_global_device_ids=true | all-gather | bytes 860160 | tf_op jit(solution)/shard_map/all_gather | solution.py:48
  1104.7 17.1 %all_gather.129 = bf16[1,448,768]{2,1,0:T(8,128)(2,1)S(1)} all-gather(bf16[1,112,768]{2,1,0:T(8,128)(2,1)S(1)} %convert_element_type.1202), channel_id=1, replica_groups=mesh['pipe'=2,'tensor'=4,'dp'=4] {'tensor'}, dimensions={1}, use_global_device_ids=true | all-gather | bytes 860160 | tf_op jit(solution)/shard_map/all_gather | solution.py:48
  1133.1 23.8 %all_gather.131 = bf16[1,448,768]{2,1,0:T(8,128)(2,1)S(1)} all-gather(bf16[1,112,768]{2,1,0:T(8,128)(2,1)S(1)} %copy-done.166), channel_id=1, replica_groups=mesh['pipe'=2,'tensor'=4,'dp'=4] {'tensor'}, dimensions={1}, use_global_device_ids=true | all-gather | bytes 860160 | tf_op jit(solution)/shard_map/all_gather | solution.py:38
  1172.4 17.2 %all_gather.132 = bf16[1,448,768]{2,1,0:T(8,128)(2,1)S(1)} all-gather(bf16[1,112,768]{2,1,0:T(8,128)(2,1)S(1)} %fusion.737), channel_id=1, replica_groups=mesh['pipe'=2,'tensor'=4,'dp'=4] {'tensor'}, dimensions={1}, use_global_device_ids=true | all-gather | bytes 860160 | tf_op jit(solution)/shard_map/all_gather | solution.py:48
  1189.6 4.6 convert_reduce_fusion
  1232.9 5.0 fusion.47
  1246.9 17.2 %all_gather.133 = bf16[1,448,768]{2,1,0:T(8,128)(2,1)S(1)} all-gather(bf16[1,112,768]{2,1,0:T(8,128)(2,1)S(1)} %convert_element_type.1229), channel_id=1, replica_groups=mesh['pipe'=2,'tensor'=4,'dp'=4] {'tensor'}, dimensions={1}, use_global_device_ids=true | all-gather | bytes 860160 | tf_op jit(solution)/shard_map/all_gather | solution.py:48
  1267.9 9.5 all-reduce.1
  1291.9 10.4 reduce-scatter.63.cloned.1.call-done
  1305.5 75.7 %all-reduce = (f32[1,2,768]{2,1,0:T(2,128)}, f32[1,2,768]{2,1,0:T(2,128)}, f32[1,2,768]{2,1,0:T(2,128)}) all-reduce(f32[1,2,768]{2,1,0:T(2,128)S(1)} %maximum_bitcast_fusion, f32[1,2,768]{2,1,0:T(2,128)S(1)} %maximum_bitcast_fusion.1, ...), channel_id=1, replica_groups=mesh['pipe'=2,'tensor'=4,'dp'=4] {'tensor','dp'}, use_global_device_ids=true, to_apply=%region_130.131 | all-reduce | flops 4608 | bytes 36864 | tf_op jit(solution)/shard_map/psum | solution.py:304
  1387.2 14.4 %all-reduce.5.cloned.1.call-done = (bf16[1,768,3,192]{1,3,2,0:T(8,128)(2,1)}, bf16[1,3,64,768]{3,2,1,0:T(8,128)(2,1)}, bf16[1,768,768]{2,1,0:T(8,128)(2,1)}, bf16[1,768,768]{2,1,0:T(8,128)(2,1)}) async-done(((bf16[1,768,3,192]{1,3,2,0:T(8,128)(2,1)}, bf16[1,3,64,768]{3,2,1,0:T(8,128)(2,1)}, bf16[1,768,768]{2,1,0:T(8,128)(2,1)}, bf16[1,768,768]{2,1,0:T(8,128)(2,1)}), (bf16[1,768,3,192]{1,3,2,0:T(8,128)(2,1)}, ...) | async-done | bytes 3538960 | tf_op jit(solution)/shard_map/psum | solution.py:295
  (1149 shorter events, 394.6 us)
Async XLA Ops:
  7.2 75.1 %copy-start = (bf16[1,768,768]{2,1,0:T(8,128)(2,1)S(1)}, bf16[1,768,768]{2,1,0:T(8,128)(2,1)}, u32[]{:S(2)}) copy-start(bf16[1,768,768]{2,1,0:T(8,128)(2,1)} %param.19) | copy-start | bytes 3538948
  7.2 24.7 %copy-start.299 = (f32[1,2,3,64]{3,1,2,0:T(2,128)S(1)}, f32[1,2,3,64]{3,1,2,0:T(2,128)}, u32[]{:S(2)}) copy-start(f32[1,2,3,64]{3,1,2,0:T(2,128)} %param.16) | copy-start | bytes 4612
  7.2 24.7 %copy-start.351 = (bf16[1,768,3,192]{1,3,2,0:T(8,128)(2,1)S(1)}, bf16[1,768,3,192]{1,3,2,0:T(8,128)(2,1)}, u32[]{:S(2)}) copy-start(bf16[1,768,3,192]{1,3,2,0:T(8,128)(2,1)} %param.15) | copy-start | bytes 2654212
  7.2 56.4 %reduce-scatter.23.cloned.1.call-start = ((), (), s32[]{:S(2)}) async-start(), calls=%async_computation.22 | async-start | bytes 860160 | tf_op jit(solution)/shard_map/reduce_scatter | solution.py:42
  10.5 23.0 %copy-start.181 = (f32[768]{0:T(1024)}, f32[768]{0:T(1024)S(1)}, u32[]{:S(2)}) copy-start(f32[768]{0:T(1024)S(1)} %get-tuple-element.64) | copy-start | bytes 9220
  37.4 26.2 %copy-start.26 = (f32[4,112,768]{2,1,0:T(8,128)S(1)}, f32[4,112,768]{2,1,0:T(8,128)}, u32[]{:S(2)}) copy-start(f32[4,112,768]{2,1,0:T(8,128)} %param.11) | copy-start | bytes 4128772
  41.1 70.4 %reduce-scatter.29.cloned.1.call-start = ((), (), s32[]{:S(2)}) async-start(), calls=%async_computation.25 | async-start | bytes 860160 | tf_op jit(solution)/shard_map/reduce_scatter | solution.py:42
  41.2 47.6 %copy-start.286 = (f32[768]{0:T(1024)}, f32[768]{0:T(1024)S(1)}, u32[]{:S(2)}) copy-start(f32[768]{0:T(1024)S(1)} %reduce.165) | copy-start | bytes 9220
  41.2 23.7 %copy-start.199 = (f32[768]{0:T(1024)}, f32[768]{0:T(1024)S(1)}, u32[]{:S(2)}) copy-start(f32[768]{0:T(1024)S(1)} %get-tuple-element.60) | copy-start | bytes 9220
  88.8 79.5 %reduce-scatter.31.cloned.1.call-start = ((), (), s32[]{:S(2)}) async-start(), calls=%async_computation.26 | async-start | bytes 860160 | tf_op jit(solution)/shard_map/reduce_scatter | solution.py:42
  112.5 3.3 collective-permute-start
  117.6 102.7 %copy-start.4 = (f32[4,1,112,768]{3,2,1,0:T(8,128)}, f32[4,1,112,768]{3,2,1,0:T(8,128)S(1)}, u32[]{:S(2)}) copy-start(f32[4,1,112,768]{3,2,1,0:T(8,128)S(1)} %get-tuple-element.114) | copy-start | bytes 4128772
  146.7 70.0 %reduce-scatter.37.cloned.1.call-start = ((), (), s32[]{:S(2)}) async-start(), calls=%async_computation.29 | async-start | bytes 860160 | tf_op jit(solution)/shard_map/reduce_scatter | solution.py:42
  193.9 79.9 %reduce-scatter.39.cloned.1.call-start = ((), (), s32[]{:S(2)}) async-start(), calls=%async_computation.30 | async-start | bytes 860160 | tf_op jit(solution)/shard_map/reduce_scatter | solution.py:42
  218.4 3.0 collective-permute-start.1
  248.3 25.5 %copy-start.200 = (f32[768]{0:T(1024)S(1)}, f32[768]{0:T(1024)}, u32[]{:S(2)}) copy-start(f32[768]{0:T(1024)} %copy-done.199) | copy-start | bytes 9220
  251.9 40.6 %copy-start.287 = (f32[768]{0:T(1024)S(1)}, f32[768]{0:T(1024)}, u32[]{:S(2)}) copy-start(f32[768]{0:T(1024)} %copy-done.286) | copy-start | bytes 9220
  251.9 74.7 %reduce-scatter.45.cloned.1.call-start = ((), (), s32[]{:S(2)}) async-start(), calls=%async_computation.33 | async-start | bytes 860160 | tf_op jit(solution)/shard_map/reduce_scatter | solution.py:42
  298.9 87.5 %reduce-scatter.47.cloned.1.call-start = ((), (), s32[]{:S(2)}) async-start(), calls=%async_computation.34 | async-start | bytes 860160 | tf_op jit(solution)/shard_map/reduce_scatter | solution.py:42
  327.7 4.6 collective-permute-start.3
  364.4 70.0 %reduce-scatter.53.cloned.1.call-start = ((), (), s32[]{:S(2)}) async-start(), calls=%async_computation.37 | async-start | bytes 860160 | tf_op jit(solution)/shard_map/reduce_scatter | solution.py:42
  366.5 50.1 %copy-start.1 = (f32[4,1,112,768]{3,2,1,0:T(8,128)}, f32[4,1,112,768]{3,2,1,0:T(8,128)S(1)}, u32[]{:S(2)}) copy-start(f32[4,1,112,768]{3,2,1,0:T(8,128)S(1)} %get-tuple-element.138) | copy-start | bytes 4128772
  411.7 169.3 %reduce-scatter.55.cloned.1.call-start = ((), (), s32[]{:S(2)}) async-start(), calls=%async_computation.38 | async-start | bytes 860160 | tf_op jit(solution)/shard_map/reduce_scatter | solution.py:42
  435.4 6.8 collective-permute-start.5
  515.3 180.7 %reduce-scatter.65.cloned.1.call-start = ((), (), s32[]{:S(2)}) async-start(), calls=%async_computation.43 | async-start | bytes 860160 | tf_op jit(solution)/shard_map/reduce_scatter | solution.py:42
  515.3 27.9 %copy-start.356 = (bf16[1,768,3,192]{1,3,2,0:T(8,128)(2,1)S(1)}, bf16[1,768,3,192]{1,3,2,0:T(8,128)(2,1)}, u32[]{:S(2)}) copy-start(bf16[1,768,3,192]{1,3,2,0:T(8,128)(2,1)} %param.15) | copy-start | bytes 2654212
  609.0 93.5 %reduce-scatter.25.cloned.1.call-start = ((), (), s32[]{:S(2)}) async-start(), calls=%async_computation.23 | async-start | bytes 860160 | tf_op jit(solution)/shard_map/reduce_scatter | solution.py:52
  631.0 28.1 %copy-start.113 = (f32[448,768]{1,0:T(8,128)}, f32[448,768]{1,0:T(8,128)S(1)}, u32[]{:S(2)}) copy-start(f32[448,768]{1,0:T(8,128)S(1)} %convolution_add_fusion.10) | copy-start | bytes 4128772
  661.5 60.2 %reduce-scatter.33.cloned.1.call-start = ((), (), s32[]{:S(2)}) async-start(), calls=%async_computation.27 | async-start | bytes 860160 | tf_op jit(solution)/shard_map/reduce_scatter | solution.py:52
  661.6 23.7 %copy-start.357 = (bf16[1,768,3,192]{1,3,2,0:T(8,128)(2,1)S(1)}, bf16[1,768,3,192]{1,3,2,0:T(8,128)(2,1)}, u32[]{:S(2)}) copy-start(bf16[1,768,3,192]{1,3,2,0:T(8,128)(2,1)} %param.15) | copy-start | bytes 2654212
  663.7 22.3 %copy-start.175 = (f32[1,448,3,192]{1,3,2,0:T(8,128)}, f32[1,448,3,192]{1,3,2,0:T(8,128)S(1)}, u32[]{:S(2)}) copy-start(f32[1,448,3,192]{1,3,2,0:T(8,128)S(1)} %convolution_bitcast_fusion.13) | copy-start | bytes 3096580
  695.9 83.5 %reduce-scatter.35.cloned.1.call-start = ((), (), s32[]{:S(2)}) async-start(), calls=%async_computation.28 | async-start | bytes 860160 | tf_op jit(solution)/shard_map/reduce_scatter | solution.py:52
  701.8 21.8 %copy-start.337 = (f32[112]{0:T(128)}, f32[112]{0:T(128)S(1)}, u32[]{:S(2)}) copy-start(f32[112]{0:T(128)S(1)} %multiply_reduce_fusion.24) | copy-start | bytes 1348
  702.0 21.6 %copy-start.341 = (f32[112]{0:T(128)S(1)}, f32[112]{0:T(128)}, u32[]{:S(2)}) copy-start(f32[112]{0:T(128)} %copy-done.340) | copy-start | bytes 1348
  702.0 21.6 %copy-start.284 = (f32[112]{0:T(128)S(1)}, f32[112]{0:T(128)}, u32[]{:S(2)}) copy-start(f32[112]{0:T(128)} %fusion.819) | copy-start | bytes 1348
  702.0 21.6 %copy-start.285 = (f32[112]{0:T(128)S(1)}, f32[112]{0:T(128)}, u32[]{:S(2)}) copy-start(f32[112]{0:T(128)} %fusion.821) | copy-start | bytes 1348
  702.0 23.7 %copy-start.278 = (f32[112]{0:T(128)}, f32[112]{0:T(128)S(1)}, u32[]{:S(2)}) copy-start(f32[112]{0:T(128)S(1)} %fusion.827) | copy-start | bytes 1348
  702.0 23.7 %copy-start.279 = (f32[112]{0:T(128)}, f32[112]{0:T(128)S(1)}, u32[]{:S(2)}) copy-start(f32[112]{0:T(128)S(1)} %fusion.825) | copy-start | bytes 1348
  702.5 23.2 %copy-start.276 = (f32[112]{0:T(128)}, f32[112]{0:T(128)S(1)}, u32[]{:S(2)}) copy-start(f32[112]{0:T(128)S(1)} %fusion.829) | copy-start | bytes 1348
  753.3 86.7 %reduce-scatter.41.cloned.1.call-start = ((), (), s32[]{:S(2)}) async-start(), calls=%async_computation.31 | async-start | bytes 860160 | tf_op jit(solution)/shard_map/reduce_scatter | solution.py:52
  783.9 9.9 collective-permute-start.2
  817.7 86.8 %reduce-scatter.43.cloned.1.call-start = ((), (), s32[]{:S(2)}) async-start(), calls=%async_computation.32 | async-start | bytes 860160 | tf_op jit(solution)/shard_map/reduce_scatter | solution.py:52
  871.8 94.0 %reduce-scatter.49.cloned.1.call-start = ((), (), s32[]{:S(2)}) async-start(), calls=%async_computation.35 | async-start | bytes 860160 | tf_op jit(solution)/shard_map/reduce_scatter | solution.py:52
  909.0 9.9 collective-permute-start.4
  918.9 22.0 %copy-start.117 = (f32[448,768]{1,0:T(8,128)}, f32[448,768]{1,0:T(8,128)S(1)}, u32[]{:S(2)}) copy-start(f32[448,768]{1,0:T(8,128)S(1)} %get-tuple-element.195) | copy-start | bytes 4128772
  918.9 22.0 %copy-start.119 = (f32[448,768]{1,0:T(8,128)}, f32[448,768]{1,0:T(8,128)S(1)}, u32[]{:S(2)}) copy-start(f32[448,768]{1,0:T(8,128)S(1)} %get-tuple-element.196) | copy-start | bytes 4128772
  943.4 87.5 %reduce-scatter.51.cloned.1.call-start = ((), (), s32[]{:S(2)}) async-start(), calls=%async_computation.36 | async-start | bytes 860160 | tf_op jit(solution)/shard_map/reduce_scatter | solution.py:52
  997.6 100.3 %reduce-scatter.57.cloned.1.call-start = ((), (), s32[]{:S(2)}) async-start(), calls=%async_computation.39 | async-start | bytes 860160 | tf_op jit(solution)/shard_map/reduce_scatter | solution.py:52
  1035.5 10.7 collective-permute-start.6
  1069.4 92.3 %reduce-scatter.59.cloned.1.call-start = ((), (), s32[]{:S(2)}) async-start(), calls=%async_computation.40 | async-start | bytes 860160 | tf_op jit(solution)/shard_map/reduce_scatter | solution.py:52
  1069.5 23.8 %copy-start.242 = (f32[3,448]{1,0:T(4,128)S(1)}, f32[3,448]{1,0:T(4,128)}, u32[]{:S(2)}) copy-start(f32[3,448]{1,0:T(4,128)} %get-tuple-element.211) | copy-start | bytes 16132
  1069.5 23.8 %copy-start.318 = (f32[3,64]{1,0:T(4,128)S(1)}, f32[3,64]{1,0:T(4,128)}, u32[]{:S(2)}) copy-start(f32[3,64]{1,0:T(4,128)} %copy-done.310) | copy-start | bytes 2308
  1129.8 110.4 %reduce-scatter.61.cloned.1.call-start = ((), (), s32[]{:S(2)}) async-start(), calls=%async_computation.41 | async-start | bytes 860160 | tf_op jit(solution)/shard_map/reduce_scatter | solution.py:52
  1129.8 27.9 %copy-start.292 = (f32[768]{0:T(1024)S(1)}, f32[768]{0:T(1024)}, u32[]{:S(2)}) copy-start(f32[768]{0:T(1024)} %copy-done.286) | copy-start | bytes 9220
  1167.2 22.3 %copy-start.350 = (bf16[1,768,768]{2,1,0:T(8,128)(2,1)S(1)}, bf16[1,768,768]{2,1,0:T(8,128)(2,1)}, u32[]{:S(2)}) copy-start(bf16[1,768,768]{2,1,0:T(8,128)(2,1)} %param.21) | copy-start | bytes 3538948
  1167.2 22.3 %copy-start.364 = (f32[448,768]{1,0:T(8,128)S(1)}, f32[448,768]{1,0:T(8,128)}, u32[]{:S(2)}) copy-start(f32[448,768]{1,0:T(8,128)} %convolution_add_fusion.1) | copy-start | bytes 4128772
  1167.2 3.4 collective-permute-start.7
  1196.7 95.2 %reduce-scatter.27.cloned.1.call-start = ((), (), s32[]{:S(2)}) async-start(), calls=%async_computation.24 | async-start | bytes 860160 | tf_op jit(solution)/shard_map/reduce_scatter | solution.py:52
  1207.6 94.7 %reduce-scatter.63.cloned.1.call-start = ((), (), s32[]{:S(2)}) async-start(), calls=%async_computation.42 | async-start | bytes 860160 | tf_op jit(solution)/shard_map/reduce_scatter | solution.py:52
  1280.8 120.8 %all-reduce.5.cloned.1.call-start = ((), (), s32[]{:S(2)}) async-start(), calls=%async_computation.44 | async-start | bytes 7077888 | tf_op jit(solution)/shard_map/psum | solution.py:295
  1303.6 77.7 %copy-start.101 = (bf16[1,112,768]{2,1,0:T(8,128)(2,1)S(1)}, bf16[1,112,768]{2,1,0:T(8,128)(2,1)}, u32[]{:S(2)}) copy-start(bf16[1,112,768]{2,1,0:T(8,128)(2,1)} %reduce-scatter.27.cloned.1.call-done) | copy-start | bytes 516100
  1305.4 77.0 %copy-start.49 = (f32[1,112,768]{2,1,0:T(8,128)S(1)}, f32[1,112,768]{2,1,0:T(8,128)}, u32[]{:S(2)}) copy-start(f32[1,112,768]{2,1,0:T(8,128)} %copy-done.47) | copy-start | bytes 1032196
  1305.4 77.0 %copy-start.53 = (f32[1,112,768]{2,1,0:T(8,128)S(1)}, f32[1,112,768]{2,1,0:T(8,128)}, u32[]{:S(2)}) copy-start(f32[1,112,768]{2,1,0:T(8,128)} %copy-done.52) | copy-start | bytes 1032196
  1305.4 77.0 %copy-start.303 = (f32[112]{0:T(128)S(1)}, f32[112]{0:T(128)}, u32[]{:S(2)}) copy-start(f32[112]{0:T(128)} %copy-done.302) | copy-start | bytes 1348
  (333 other events, 1684.1 us)
Sparse Core Ops, SparseCore 0:
  41.2 22.3 reduce-scatter.22
  88.9 22.5 reduce-scatter.28
  146.9 21.3 reduce-scatter.30
  194.1 22.6 reduce-scatter.36
  252.0 21.7 reduce-scatter.38
  299.0 26.5 reduce-scatter.44
  364.5 21.8 reduce-scatter.46
  411.8 22.5 reduce-scatter.52
  515.4 30.2 reduce-scatter.54
  609.1 25.2 reduce-scatter.64
  661.7 26.7 reduce-scatter.24
  696.0 25.6 reduce-scatter.32
  753.4 25.9 reduce-scatter.34
  817.8 22.1 reduce-scatter.40
  871.9 28.7 reduce-scatter.42
  943.5 22.2 reduce-scatter.48
  997.7 27.6 reduce-scatter.50
  1069.5 27.3 reduce-scatter.56
  1129.9 28.7 reduce-scatter.58
  1196.8 22.1 reduce-scatter.60
  1221.3 21.3 reduce-scatter.26
  1280.9 21.3 reduce-scatter.62
  1306.9 94.6 all-reduce.4
where the time goes:
time: 1430 us; the launch traced here: 1420 us
  blocking collectives  703 us (49%)
  matrix products  271 us (19%)
  waiting for transfers between devices  202 us (14%)
  other arithmetic  149 us (10%)
  local copies, waits for them, and re-layouts  58 us (4%)
  between operations  18.5 us (1%)
    all_gather x22, blocking collectives, gather_normed(): return lax.all_gather(normed, 'tensor', axis=1, tiled=True)  417 us
    all_gather x11, blocking collectives, gather_grads(): lax.all_gather(grad_rows.astype(jnp.bfloat16), 'tensor', axis=1, tiled=True)  200 us
    reduce_scatter x10, waiting for transfers between devices, sum_branch(): lax.psum_scatter(pieces.astype(jnp.bfloat16), 'tensor', scatter_dimension...  139 us
    psum x1, blocking collectives, per_device(): lax.psum((gain_stack, shift_stack, bias_stack), ('tensor', 'dp'))  75.7 us
    unnamed x743, local copies, waits for them, and re-layouts  49.4 us
    reduce_scatter x12, waiting for transfers between devices, sum_normed_grads(): lax.psum_scatter(pieces.astype(jnp.bfloat16), 'tensor', scatter_dimension...  47 us
    sub x11, matrix products, softmax_rows(): powers = jnp.exp(scores - row_peak)  45.8 us
    dot_general x5, matrix products, per_device(): jnp.dot(forward_active, down_matrix, preferred_element_type=f32)  32.5 us
  transfers between devices with their start and end apart: 31, of which 14 were waited for; matrix products, arithmetic and copies ran while one was open for 16% of the time, Pallas kernels for 0%

commit v1 on v0

v1 whole, which is shorter than its diff:
```python
import functools

import jax
import jax.numpy as jnp
from jax import lax
from jax.experimental import pallas as pl
from jax.experimental.pallas import tpu as pltpu
from jax.sharding import PartitionSpec as P

EPSILON = 1e-05
MESH = pl.DeviceIdType.MESH
f32 = jnp.float32
bf16 = jnp.bfloat16


def swap_pipe(block):
    return lax.ppermute(block, "pipe", [(0, 1), (1, 0)])


def norm_stats(values):
    row_mean = jnp.mean(values, axis=-1, keepdims=True)
    centered = values - row_mean
    variance = jnp.mean(centered * centered, axis=-1, keepdims=True)
    scale = lax.rsqrt(variance + EPSILON)
    return centered * scale, scale


def norm_back(normed_grad, values, gain_row):
    normed, scale = norm_stats(values)
    scaled = normed_grad * gain_row
    return scale * (
        scaled
        - jnp.mean(scaled, axis=-1, keepdims=True)
        - normed * jnp.mean(scaled * normed, axis=-1, keepdims=True)
    )


def exact_gelu(values):
    return jax.nn.gelu(values, approximate=False)


def greet(peers):
    barrier = pltpu.get_barrier_semaphore()
    for peer in peers:
        pl.semaphore_signal(barrier, inc=1, device_id={"tensor": peer}, device_id_type=MESH)
    pl.semaphore_wait(barrier, len(peers))


def remote(src, dst, send_sem, recv_sem, peer):
    return pltpu.make_async_remote_copy(
        src_ref=src,
        dst_ref=dst,
        send_sem=send_sem,
        recv_sem=recv_sem,
        device_id={"tensor": peer},
        device_id_type=MESH,
    )


def peers_of(group):
    me = lax.axis_index("tensor")
    return me, [lax.rem(me + k, group) for k in range(1, group)]


def gather_kernel(group, value_ref, gain_ref, shift_ref, full_ref, own, send_sem, recv_sem):
    me, peers = peers_of(group)
    greet(peers)
    copies = []
    for c in range(value_ref.shape[0]):
        normed, _ = norm_stats(value_ref[c])
        own[c] = (normed * gain_ref[...] + shift_ref[...]).astype(bf16)
        for k, peer in enumerate(peers):
            copy = remote(
                own.at[c], full_ref.at[c, me], send_sem.at[c, k], recv_sem.at[c, k], peer
            )
            copy.start()
            copies.append(copy)
        full_ref[c, me] = own[c]
    for copy in copies:
        copy.wait()


def exchange_kernel(group, transpose, mode, *refs):
    if mode == "forward":
        act, weight, resid, bias, gain, shift, value_out, full_out, *scratch = refs
    elif mode == "backward":
        act, weight, resid, saved, gain, sum_out, value_out, full_out, *scratch = refs
    else:
        act, weight, sum_out, *scratch = refs
    if mode == "sum":
        pieces, landed, send_sem, recv_sem = scratch
    else:
        pieces, landed, own, send_sem, recv_sem, send_two, recv_two = scratch
    me, peers = peers_of(group)
    clips = act.shape[0]
    contract = (((1,), (1,)), ((), ())) if transpose else (((1,), (0,)), ((), ()))

    def product(c, j):
        return lax.dot_general(act[c, j], weight[...], contract, preferred_element_type=f32)

    greet(peers)
    copies = {}
    for c in range(clips):
        for k, peer in enumerate(peers):
            pieces[c, k] = product(c, peer).astype(bf16)
            copies[c, k] = remote(
                pieces.at[c, k], landed.at[c, k], send_sem.at[c, k], recv_sem.at[c, k], peer
            )
            copies[c, k].start()
    waits = []
    for c in range(clips):
        total = product(c, me)
        for k in range(group - 1):
            copies[c, k].wait()
            total = total + landed[c, k].astype(f32)
        if mode == "sum":
            sum_out[c] = total
            continue
        if mode == "forward":
            value = resid[c] + total + bias[...]
            value_out[c] = value
            normed, _ = norm_stats(value)
            own[c] = (normed * gain[...] + shift[...]).astype(bf16)
        else:
            sum_out[c] = total
            value = resid[c] + norm_back(total, saved[c], gain[...])
            value_out[c] = value
            own[c] = value.astype(bf16)
        for k, peer in enumerate(peers):
            copy = remote(
                own.at[c], full_out.at[c, me], send_two.at[c, k], recv_two.at[c, k], peer
            )
            copy.start()
            waits.append(copy)
        full_out[c, me] = own[c]
    for copy in waits:
        copy.wait()


VMEM = pl.BlockSpec(memory_space=pltpu.VMEM)
DMA = pltpu.SemaphoreType.DMA


def params(number):
    return pltpu.CompilerParams(
        collective_id=number, has_side_effects=True, vmem_limit_bytes=40 * 1024 * 1024
    )


def gather_normed(rows, gain, shift):
    group = lax.axis_size("tensor")
    clips, share, width = rows.shape
    full = pl.pallas_call(
        functools.partial(gather_kernel, group),
        out_shape=jax.ShapeDtypeStruct((clips, group, share, width), bf16),
        in_specs=[VMEM] * 3,
        out_specs=VMEM,
        scratch_shapes=[
            pltpu.VMEM((clips, share, width), bf16),
            DMA((clips, group - 1)),
            DMA((clips, group - 1)),
        ],
        compiler_params=params(0),
        name="gather_normed",
    )(rows, gain[None], shift[None])
    return full.reshape(clips * group * share, width)


def exchange(mode, number, act, weight, transpose, share, *rest):
    group = lax.axis_size("tensor")
    width = weight.shape[0] if transpose else weight.shape[1]
    depth = act.shape[-1]
    act = act.reshape(-1, group, share, depth)
    clips = act.shape[0]
    rows = jax.ShapeDtypeStruct((clips, share, width), f32)
    full = jax.ShapeDtypeStruct((clips, group, share, width), bf16)
    outs = {"forward": (rows, full), "backward": (rows, rows, full), "sum": (rows,)}[mode]
    sems = [DMA((clips, group - 1)), DMA((clips, group - 1))]
    block = pltpu.VMEM((clips, group - 1, share, width), bf16)
    scratch = [block, block]
    if mode != "sum":
        scratch = scratch + [pltpu.VMEM((clips, share, width), bf16)] + sems
    scratch = scratch + sems
    rest = tuple(item[None] if item.ndim == 1 else item for item in rest)
    got = pl.pallas_call(
        functools.partial(exchange_kernel, group, transpose, mode),
        out_shape=outs,
        in_specs=[VMEM] * (2 + len(rest)),
        out_specs=tuple(VMEM for _ in outs),
        scratch_shapes=scratch,
        compiler_params=params(number),
        name=mode + "_exchange",
    )(act, weight, *rest)
    if mode == "sum":
        return got[0]
    return got[:-1] + (got[-1].reshape(clips * group * share, width),)


def shifted(block, distance):
    size = lax.axis_size("tensor")
    return lax.ppermute(block, "tensor", [(i, (i + distance) % size) for i in range(size)])


def gather_rows(block):
    size = lax.axis_size("tensor")
    me = lax.axis_index("tensor")
    clips, share, width = block.shape
    full = jnp.zeros((clips, size, share, width), block.dtype)
    for k in range(size):
        part = block if k == 0 else shifted(block, k)
        full = lax.dynamic_update_slice(full, part[:, None], (0, (me - k) % size, 0, 0))
    return full.reshape(clips * size * share, width)


def sum_rows(pieces):
    size = lax.axis_size("tensor")
    me = lax.axis_index("tensor")
    total = None
    for k in range(size):
        part = lax.dynamic_index_in_dim(pieces, (me + k) % size, 1, keepdims=False)
        part = part if k == 0 else shifted(part, k)
        total = part.astype(f32) if total is None else total + part.astype(f32)
    return total


def per_device(
    features,
    cotangent,
    norm_gains,
    norm_shifts,
    qkv_weight,
    qv_bias,
    out_weight,
    out_bias,
    up_weight,
    up_bias,
    down_weight,
):
    section = lax.axis_index("pipe")
    leading = section == 0
    share, width = features.shape[1:]
    group = lax.axis_size("tensor")
    length = share * group
    heads = qkv_weight.shape[2]
    hdim = qv_bias.shape[3]
    hidden = up_weight.shape[2]
    scale = hdim ** (-0.5)
    half = features.shape[0] // 2

    def both(block):
        other = swap_pipe(block)
        return jnp.where(leading, block, other), jnp.where(leading, other, block)

    qkv = both(qkv_weight[0].reshape(width, heads * 3 * hdim))
    out = both(out_weight[0].reshape(heads * hdim, width))
    up = both(up_weight[0])
    down = both(down_weight[0])
    small = [norm_gains, norm_shifts, qv_bias, out_bias, up_bias]
    packed = jnp.concatenate([item.reshape(-1) for item in small])
    unpacked = []
    for vector in both(packed):
        at, parts = 0, []
        for item in small:
            parts.append(vector[at : at + item.size].reshape(item.shape[1:]))
            at += item.size
        unpacked.append(parts)

    rows = lax.dynamic_slice_in_dim(features, section * half, half, 0)
    top_grad = lax.dynamic_slice_in_dim(cotangent, section * half, half, 0)
    grads_full = gather_rows(top_grad.astype(bf16))

    entries, middles, gathered, gathered_two, attn, mlp = [], [], [], [], [], []
    full = gather_normed(rows, unpacked[0][0][0], unpacked[0][1][0])
    for l in range(2):
        gain, shift, qv, ends, up_vector = unpacked[l]
        entries.append(rows)
        gathered.append(full)
        projected = jnp.dot(full, qkv[l], preferred_element_type=f32)
        projected = projected.reshape(half, length, heads, 3 * hdim)
        queries = (projected[..., :hdim] + qv[0]).astype(bf16)
        keys = projected[..., hdim : 2 * hdim].astype(bf16)
        values = (projected[..., 2 * hdim :] + qv[1]).astype(bf16)
        scores = jnp.einsum("bqhe,bkhe->bhqk", queries, keys, preferred_element_type=f32) * scale
        powers = jnp.exp(scores - jnp.max(scores, axis=-1, keepdims=True))
        prob = powers / jnp.sum(powers, axis=-1, keepdims=True)
        prob_low = prob.astype(bf16)
        attended = jnp.einsum("bhqk,bkhe->bqhe", prob_low, values, preferred_element_type=f32)
        attended = attended.astype(bf16).reshape(half * length, heads * hdim)
        attn.append((queries, keys, values, prob, prob_low, attended))
        middle, full = exchange(
            "forward", 1, attended, out[l], False, share, rows, ends[0], gain[1], shift[1]
        )
        middles.append(middle)
        gathered_two.append(full)
        pre = jnp.dot(full, up[l], preferred_element_type=f32) + up_vector
        active = exact_gelu(pre).astype(bf16)
        mlp.append((pre, active))
        if l == 0:
            rows, full = exchange(
                "forward", 2, active, down[l], False, share, middle, ends[1],
                unpacked[1][0][0], unpacked[1][1][0],
            )
        else:
            pieces = jnp.dot(active, down[l], preferred_element_type=f32).astype(bf16)
            pieces = pieces.reshape(half, group, share, width)
            result = middle + sum_rows(pieces) + ends[1]

    layer_grads = [None, None]
    shared = [None, None]
    incoming = top_grad
    for l in (1, 0):
        gain, shift, qv, ends, up_vector = unpacked[l]
        pre, active = mlp[l]
        down_grad = jnp.einsum("nf,nd->fd", active, grads_full, preferred_element_type=f32)
        active_grad = jnp.einsum("nd,fd->nf", grads_full, down[l], preferred_element_type=f32)
        pre_grad = jax.vjp(exact_gelu, pre)[1](active_grad)[0].astype(bf16)
        up_bias_grad = jnp.sum(pre_grad.astype(f32), axis=0)
        up_grad = jnp.einsum("nd,nf->df", gathered_two[l], pre_grad, preferred_element_type=f32)
        sum_two, middle_grad, full = exchange(
            "backward", 3, pre_grad, up[l], True, share, incoming, middles[l], gain[1]
        )
        normed_two = norm_stats(middles[l])[0]
        queries, keys, values, prob, prob_low, attended = attn[l]
        out_grad = jnp.einsum("nc,nd->cd", attended, full, preferred_element_type=f32)
        attended_grad = jnp.einsum("nd,cd->nc", full, out[l], preferred_element_type=f32)
        attended_grad = attended_grad.astype(bf16).reshape(half, length, heads, hdim)
        prob_grad = jnp.einsum(
            "bqhe,bkhe->bhqk", attended_grad, values, preferred_element_type=f32
        )
        values_grad = jnp.einsum(
            "bhqk,bqhe->bkhe", prob_low, attended_grad, preferred_element_type=f32
        ).astype(bf16)
        inner = jnp.sum(prob * prob_grad, axis=-1, keepdims=True)
        scores_grad = (prob * (prob_grad - inner)).astype(bf16)
        queries_grad = (
            jnp.einsum("bhqk,bkhe->bqhe", scores_grad, keys, preferred_element_type=f32) * scale
        ).astype(bf16)
        keys_grad = (
            jnp.einsum("bhqk,bqhe->bkhe", scores_grad, queries, preferred_element_type=f32) * scale
        ).astype(bf16)
        flat = jnp.concatenate([queries_grad, keys_grad, values_grad], axis=-1)
        flat = flat.reshape(half * length, heads * 3 * hdim)
        bias_grad = jnp.stack(
            [
                jnp.sum(queries_grad.astype(f32), axis=(0, 1)),
                jnp.sum(values_grad.astype(f32), axis=(0, 1)),
            ]
        )
        qkv_grad = jnp.einsum("nd,nc->dc", gathered[l], flat, preferred_element_type=f32)
        end_grads = [jnp.sum(middle_grad, axis=(0, 1)), jnp.sum(incoming, axis=(0, 1))]
        if l == 1:
            sum_one, entry_grad, grads_full = exchange(
                "backward", 4, flat, qkv[l], True, share, middle_grad, entries[l], gain[0]
            )
        else:
            sum_one = exchange("sum", 5, flat, qkv[l], True, share)
            entry_grad = middle_grad + norm_back(sum_one, entries[l], gain[0])
        normed_one = norm_stats(entries[l])[0]
        shared[l] = jnp.stack(
            [
                jnp.sum(sum_one * normed_one, axis=(0, 1)),
                jnp.sum(sum_two * normed_two, axis=(0, 1)),
                jnp.sum(sum_one, axis=(0, 1)),
                jnp.sum(sum_two, axis=(0, 1)),
            ]
            + end_grads
        )
        layer_grads[l] = (
            qkv_grad,
            out_grad,
            up_grad,
            down_grad,
            jnp.concatenate([bias_grad.reshape(-1), up_bias_grad]),
        )
        incoming = entry_grad

    def reduced(first, second):
        mine = jnp.where(leading, first, second)
        other = jnp.where(leading, second, first)
        return mine + swap_pipe(other.astype(bf16)).astype(f32)

    summed = [
        lax.psum(reduced(a, b).astype(bf16), "dp").astype(f32) for a, b in zip(*layer_grads)
    ]
    common = jnp.where(leading, shared[0], shared[1]) + swap_pipe(
        jnp.where(leading, shared[1], shared[0])
    )
    common = lax.psum(common, ("tensor", "dp"))
    given = swap_pipe(jnp.where(leading, result, entry_grad))
    boundary = jnp.where(
        leading,
        jnp.concatenate([entry_grad, given]),
        jnp.concatenate([given, result]),
    )
    bias_size = 2 * heads * hdim
    return (
        boundary[None],
        common[None, 0:2],
        common[None, 2:4],
        summed[0].reshape(1, width, heads, 3 * hdim),
        summed[4][:bias_size].reshape(1, 2, heads, hdim),
        summed[1].reshape(1, heads, hdim, width),
        common[None, 4:6],
        summed[2][None],
        summed[4][bias_size:][None],
        summed[3][None],
    )


def solution(mesh):
    in_specs = (
        P("dp", "tensor", None),
        P("dp", "tensor", None),
        P("pipe", None, None),
        P("pipe", None, None),
        P("pipe", None, "tensor", None),
        P("pipe", None, "tensor", None),
        P("pipe", "tensor", None, None),
        P("pipe", None, None),
        P("pipe", None, "tensor"),
        P("pipe", "tensor"),
        P("pipe", "tensor", None),
    )
    out_specs = (
        P("pipe", "dp", "tensor", None),
        P("pipe", None, None),
        P("pipe", None, None),
        P("pipe", None, "tensor", None),
        P("pipe", None, "tensor", None),
        P("pipe", "tensor", None, None),
        P("pipe", None, None),
        P("pipe", None, "tensor"),
        P("pipe", "tensor"),
        P("pipe", "tensor", None),
    )
    return jax.shard_map(
        per_device, mesh=mesh, in_specs=in_specs, out_specs=out_specs, check_vma=False
    )
```

time: 1430 us -> 844 us (0.59)
  blocking collectives: 703 us -> 84.7 us
  Pallas kernels: 0 us -> 456 us
  waiting for transfers between devices: 202 us -> 28.8 us
  matrix products: 271 us -> 99.6 us
  other arithmetic: 149 us -> 47.6 us
  local copies, waits for them, and re-layouts: 58 us -> 85.6 us
    all_gather x33 -> x0, blocking collectives: 617 us -> none  [the longest x22 417 us: gather_normed(): return lax.all_gather(normed, 'tensor', axis=1, tiled=True)]
    pallas_call x0 -> x8, Pallas kernels: none -> 456 us  [the longest x7 409 us: exchange(): pl.pallas_call(functools.partial(exchange_kernel, group, transpose, mode)...]
    reduce_scatter x22 -> x0, waiting for transfers between devices: 186 us -> none  [the longest x10 139 us: sum_branch(): lax.psum_scatter(pieces.astype(jnp.bfloat16), 'tensor', scatter_dimension...]
    dot_general x104 -> x27, matrix products: 225 us -> 88.3 us  [the longest x2 18.8 us: per_device(): pre = jnp.dot(full, up[l], preferred_element_type=f32) + up_vector]
    reduce_sum x58 -> x12, other arithmetic: 64.5 us -> 4.29 us  [the longest x4 1.59 us: norm_stats(): row_mean = jnp.mean(values, axis=-1, keepdims=True)]
    sub x11 -> x2, matrix products: 45.8 us -> 11.4 us  [per_device(): powers = jnp.exp(scores - jnp.max(scores, axis=-1, keepdims=True))]
    ppermute x8 -> x18, waiting for transfers between devices: 1.47 us -> 28.8 us  [the longest x6 28.8 us: shifted(): lax.ppermute(block, 'tensor', [(i, (i + distance) % size) for i in range(...]
    unnamed x743 -> x174, local copies, waits for them, and re-layouts: 49.4 us -> 22.8 us
  transfers between devices with their start and end apart: 31 -> 19, of which waited for: 14 -> 3; matrix products, arithmetic and copies ran while one was open for 16% -> 14% of each run, Pallas kernels for 0% -> 17%
where the time goes in v1:
time: 844 us; the launch traced here: 834 us
  Pallas kernels  456 us (54%)
  matrix products  99.6 us (12%)
  local copies, waits for them, and re-layouts  85.6 us (10%)
  blocking collectives  84.7 us (10%)
  other arithmetic  47.6 us (6%)
  waiting for transfers between devices  28.8 us (3%)
  starting transfers between devices  15.7 us (2%)
  between operations  15.7 us (2%)
    pallas_call x7, Pallas kernels, exchange(): pl.pallas_call(functools.partial(exchange_kernel, group, transpose, mode)...  409 us
    psum x1, blocking collectives, per_device(): common = lax.psum(common, ('tensor', 'dp'))  74.6 us
    pallas_call x1, Pallas kernels, gather_normed(): pl.pallas_call(functools.partial(gather_kernel, group), out_shape=jax.Sha...  47.5 us
    ppermute x6, waiting for transfers between devices, shifted(): lax.ppermute(block, 'tensor', [(i, (i + distance) % size) for i in range(...  28.8 us
    unnamed x174, local copies, waits for them, and re-layouts  22.8 us
    another operation x8, local copies, waits for them, and re-layouts, exchange(): act = act.reshape(-1, group, share, depth)  20.6 us
    dot_general x2, matrix products, per_device(): pre = jnp.dot(full, up[l], preferred_element_type=f32) + up_vector  18.8 us
  transfers between devices with their start and end apart: 19, of which 3 were waited for; matrix products, arithmetic and copies ran while one was open for 14% of the time, Pallas kernels for 17%

profile of v1, /device:TPU:0, one launch (start us, length us, event | category | flops | bytes accessed | tf_op | source)
XLA Modules:
  0.0 834.1 jit_solution(4484422894541532526)
XLA Ops:
  8.7 3.1 collective-permute-start.5
  11.7 2.6 collective-permute-start.6
  18.5 2.2 copy.123
  22.5 47.5 %gather_normed.1 = bf16[2,4,112,768]{3,2,1,0:T(8,128)(2,1)S(1)} custom-call(f32[2,112,768]{2,1,0:T(8,128)S(1)} %get-tuple-element.92.value_ref.refs_2_, f32[1,768]{1,0:T(1,128)S(1)} %slice.214.gain_ref, f32[1,768]{1,0:T(1,128)S(1)} %slice.216.shift_ref), custom_call_target="tpu_custom_call" | custom-call | tf_op jit(solution)/shard_map/gather_normed/pallas_call | solution.py:153
  77.6 2.2 copy.124
  83.1 4.1 fusion.113
  87.2 5.6 fusion.103
  92.8 3.5 fusion.55
  97.7 2.0 copy.127.refs_0_
  104.0 63.1 %forward_exchange.3 = (f32[2,112,768]{2,1,0:T(8,128)S(1)}, bf16[2,4,112,768]{3,2,1,0:T(8,128)(2,1)S(1)}) custom-call(bf16[2,4,112,192]{3,2,1,0:T(8,128)(2,1)S(1)} %copy-done.25, bf16[192,768]{1,0:T(8,128)(2,1)S(1)} %copy-done.19, f32[2,112,768]{2,1,0:T(8,128)S(1)} %get-tuple-element.92.value_ref.refs_2_, f32[1,768]{1,0:T(1,128)S(1)} %slice.225.refs_3_, ...), custom_call_target="tpu_custom_call" | custom-call | tf_op jit(solution)/shard_map/forward_exchange/pallas_call | solution.py:185
  168.2 2.9 broadcast_select_fusion.1
  171.1 8.9 %multiply_convert_fusion.3 = (bf16[896,768]{1,0:T(8,128)(2,1)S(1)}, f32[896,768]{1,0:T(8,128)}, f32[896,768]{1,0:T(8,128)}) fusion(f32[768]{0:T(1024)S(1)} %get-tuple-element.125, bf16[896,768]{1,0:T(8,128)(2,1)S(1)} %bitcast.191, bf16[768,768]{1,0:T(8,128)(2,1)S(1)} %get-tuple-element.100.refs_1_), kind=kOutput, calls=%fused_computation.34 | convolution fusion | flops 1102381056 | bytes 9440256 | tf_op jit(solution)/shard_map/dot_general | solution.py:295
  180.0 1.9 broadcast_select_fusion.2.refs_1_
  181.9 62.6 %forward_exchange.4 = (f32[2,112,768]{2,1,0:T(8,128)S(1)}, bf16[2,4,112,768]{3,2,1,0:T(8,128)(2,1)S(1)}) custom-call(bf16[2,4,112,768]{3,2,1,0:T(8,128)(2,1)S(1)} %bitcast.187, bf16[768,768]{1,0:T(8,128)(2,1)S(1)} %broadcast_select_fusion.2.refs_1_, f32[2,112,768]{2,1,0:T(8,128)S(1)} %get-tuple-element.26.refs_2_.refs_3_, f32[1,768]{1,0:T(1,128)S(1)} %slice.232.refs_3_, ...), custom_call_target="tpu_custom_call" | custom-call | tf_op jit(solution)/shard_map/forward_exchange/pallas_call | solution.py:185
  246.8 2.5 fusion.114
  249.3 5.7 fusion.104
  255.0 3.5 fusion.49
  259.5 2.0 copy.132.refs_0_
  263.5 62.3 %forward_exchange.5 = (f32[2,112,768]{2,1,0:T(8,128)S(1)}, bf16[2,4,112,768]{3,2,1,0:T(8,128)(2,1)S(1)}) custom-call(bf16[2,4,112,192]{3,2,1,0:T(8,128)(2,1)S(1)} %copy-done.26, bf16[192,768]{1,0:T(8,128)(2,1)S(1)} %copy-done.21, f32[2,112,768]{2,1,0:T(8,128)S(1)} %get-tuple-element.28.refs_2_.refs_3_, f32[1,768]{1,0:T(1,128)S(1)} %slice.245.refs_3_, ...), custom_call_target="tpu_custom_call" | custom-call | tf_op jit(solution)/shard_map/forward_exchange/pallas_call | solution.py:185
  325.8 9.9 %multiply_convert_fusion.2 = (bf16[896,768]{1,0:T(8,128)(2,1)}, f32[896,768]{1,0:T(8,128)S(1)}, f32[896,768]{1,0:T(8,128)S(1)}) fusion(f32[768]{0:T(1024)S(1)} %get-tuple-element.116, bf16[896,768]{1,0:T(8,128)(2,1)S(1)} %bitcast.183, bf16[768,768]{1,0:T(8,128)(2,1)} %get-tuple-element.99.refs_1_), kind=kOutput, calls=%fused_computation.18 | convolution fusion | flops 1102381056 | bytes 9440256 | tf_op jit(solution)/shard_map/dot_general | solution.py:295
  335.7 3.8 convert_reduce_fusion
  339.5 61.7 %backward_exchange.3 = (f32[2,112,768]{2,1,0:T(8,128)S(1)}, f32[2,112,768]{2,1,0:T(8,128)S(1)}, bf16[2,4,112,768]{3,2,1,0:T(8,128)(2,1)S(1)}) custom-call(bf16[2,4,112,768]{3,2,1,0:T(8,128)(2,1)S(1)} %bitcast.182, bf16[768,768]{1,0:T(8,128)(2,1)S(1)} %copy-done.11, f32[2,112,768]{2,1,0:T(8,128)S(1)} %get-tuple-element.87.refs_2_, ...), custom_call_target="tpu_custom_call" | custom-call | tf_op jit(solution)/shard_map/backward_exchange/pallas_call | solution.py:185
  405.8 4.1 multiply_reduce_fusion.1
  409.9 4.2 multiply_convert_fusion.1
  415.8 3.6 convert_reduce_fusion.2
  421.9 3.9 reshape_reshape.14
  425.8 3.6 copy.142.refs_0_
  431.9 62.6 %backward_exchange.4 = (f32[2,112,768]{2,1,0:T(8,128)S(1)}, f32[2,112,768]{2,1,0:T(8,128)S(1)}, bf16[2,4,112,768]{3,2,1,0:T(8,128)(2,1)S(1)}) custom-call(bf16[2,4,112,576]{3,2,1,0:T(8,128)(2,1)S(1)} %copy-done.14, bf16[768,576]{1,0:T(8,128)(2,1)S(1)} %copy-done.1, f32[2,112,768]{2,1,0:T(8,128)S(1)} %copy-done.17, ...), custom_call_target="tpu_custom_call" | custom-call | tf_op jit(solution)/shard_map/backward_exchange/pallas_call | solution.py:185
  494.6 2.9 fusion.118
  498.9 2.0 convert_reduce_fusion.1
  500.9 2.9 fusion.117
  503.8 62.7 %backward_exchange.5 = (f32[2,112,768]{2,1,0:T(8,128)S(1)}, f32[2,112,768]{2,1,0:T(8,128)S(1)}, bf16[2,4,112,768]{3,2,1,0:T(8,128)(2,1)S(1)}) custom-call(bf16[2,4,112,768]{3,2,1,0:T(8,128)(2,1)S(1)} %bitcast.188, bf16[768,768]{1,0:T(8,128)(2,1)S(1)} %copy-done.10, f32[2,112,768]{2,1,0:T(8,128)S(1)} %get-tuple-element.34.refs_2_, ...), custom_call_target="tpu_custom_call" | custom-call | tf_op jit(solution)/shard_map/backward_exchange/pallas_call | solution.py:185
  570.6 2.1 reshape.336
  572.6 4.3 multiply_reduce_fusion
  576.9 4.2 multiply_convert_fusion
  584.2 4.4 convert_reduce_fusion.4
  588.7 2.2 copy.151
  590.9 3.3 select_convert_fusion
  594.3 3.3 select_convert_fusion.1
  598.9 2.0 reshape.347
  601.0 2.9 select_convert_fusion.3
  605.7 2.2 copy.150
  608.0 3.9 reshape.339
  611.8 4.1 reshape.341
  615.9 3.2 fusion.115
  619.2 3.0 select_convert_fusion.2
  622.2 2.2 copy.156
  625.1 4.4 convolution_convert_fusion
  629.5 3.8 reshape_reshape.15
  636.2 3.3 copy.148.refs_0_
  641.9 33.8 %sum_exchange.1 = f32[2,112,768]{2,1,0:T(8,128)S(1)} custom-call(bf16[2,4,112,576]{3,2,1,0:T(8,128)(2,1)S(1)} %copy-done.15, bf16[768,576]{1,0:T(8,128)(2,1)S(1)} %copy-done.3), custom_call_target="tpu_custom_call" | custom-call | tf_op jit(solution)/shard_map/sum_exchange/pallas_call | solution.py:185
  677.5 2.5 copy.157
  680.0 3.3 add_convert_fusion.4
  683.4 2.2 copy.158
  685.6 3.6 fusion.63
  689.2 2.7 fusion.62
  693.3 4.2 collective-permute-start.10
  699.9 6.1 collective-permute-done.10
  706.0 8.0 collective-permute-done.8
  714.0 14.6 %collective-permute-done.9 = bf16[2,112,768]{2,1,0:T(8,128)(2,1)S(1)} collective-permute-done((bf16[2,112,768]{2,1,0:T(8,128)(2,1)S(1)}, bf16[2,112,768]{2,1,0:T(8,128)(2,1)S(1)}, u32[]{:S(2)}, u32[]{:S(2)}) %collective-permute-start.9) | collective-permute-done | bytes 344096 | tf_op jit(solution)/shard_map/ppermute | solution.py:201
  728.7 2.6 broadcast_select_fusion.10
  732.2 10.1 %psum.44 = bf16[1152]{0:T(1024)(128)(2,1)S(1)} all-reduce(bf16[1152]{0:T(1024)(128)(2,1)S(1)} %add_convert_fusion.6), channel_id=1, replica_groups=mesh['pipe'=2,'tensor'=4,'dp'=4] {'dp'}, use_global_device_ids=true, to_apply=%region_36.37 | all-reduce | flops 1152 | bytes 4608 | tf_op jit(solution)/shard_map/psum | solution.py:383
  743.6 74.6 %psum.42 = f32[6,768]{1,0:T(8,128)S(1)} all-reduce(f32[6,768]{1,0:T(8,128)S(1)} %select_add_fusion), channel_id=1, replica_groups=mesh['pipe'=2,'tensor'=4,'dp'=4] {'tensor','dp'}, use_global_device_ids=true, to_apply=%region_28.29 | all-reduce | flops 4608 | bytes 36864 | tf_op jit(solution)/shard_map/psum | solution.py:388
  820.0 3.0 broadcast_in_dim.69
  (314 shorter events, 72.2 us)
Async XLA Ops:
  7.2 8.5 %copy-start.77 = (f32[1,2,768]{2,1,0:T(2,128)S(1)}, f32[1,2,768]{2,1,0:T(2,128)}, u32[]{:S(2)}) copy-start(f32[1,2,768]{2,1,0:T(2,128)} %param.13) | copy-start | bytes 18436
  7.2 8.5 %copy-start.78 = (f32[1,2,768]{2,1,0:T(2,128)S(1)}, f32[1,2,768]{2,1,0:T(2,128)}, u32[]{:S(2)}) copy-start(f32[1,2,768]{2,1,0:T(2,128)} %param.14) | copy-start | bytes 18436
  7.2 8.5 %copy-start.80 = (f32[1,2,3,64]{3,1,2,0:T(2,128)S(1)}, f32[1,2,3,64]{3,1,2,0:T(2,128)}, u32[]{:S(2)}) copy-start(f32[1,2,3,64]{3,1,2,0:T(2,128)} %param.16) | copy-start | bytes 4612
  7.2 8.6 %copy-start.79 = (f32[1,2,768]{2,1,0:T(2,128)S(1)}, f32[1,2,768]{2,1,0:T(2,128)}, u32[]{:S(2)}) copy-start(f32[1,2,768]{2,1,0:T(2,128)} %param.18) | copy-start | bytes 18436
  7.2 8.7 %copy-start.81 = (f32[1,768]{1,0:T(1,128)S(1)}, f32[1,768]{1,0:T(1,128)}, u32[]{:S(2)}) copy-start(f32[1,768]{1,0:T(1,128)} %param.20) | copy-start | bytes 9220
  7.2 812.8 %all-reduce.3.cloned.1.call-start = ((), (), s32[]{:S(2)}) async-start(), calls=%async_computation | async-start | bytes 7077888 | tf_op jit(solution)/shard_map/psum | solution.py:383
  8.6 12.8 %copy-start.69 = (bf16[1,3,64,768]{3,2,1,0:T(8,128)(2,1)S(1)}, bf16[1,3,64,768]{3,2,1,0:T(8,128)(2,1)}, u32[]{:S(2)}) copy-start(bf16[1,3,64,768]{3,2,1,0:T(8,128)(2,1)} %param.17) | copy-start | bytes 884740
  8.7 64.3 %collective-permute-start.5 = (bf16[2,112,768]{2,1,0:T(8,128)(2,1)S(1)}, bf16[2,112,768]{2,1,0:T(8,128)(2,1)}, u32[]{:S(2)}, u32[]{:S(2)}) collective-permute-start(bf16[2,112,768]{2,1,0:T(8,128)(2,1)S(1)} %get-tuple-element.94), channel_id=1, source_target_pairs={{0,4},{4,8},{8,12},{12,0},{1,5},{5,9},{9,13},{13,1},{2,6},{6,10},{... | collective-permute-start | bytes 1032200 | tf_op jit(solution)/shard_map/ppermute | solution.py:201
  11.7 62.7 %collective-permute-start.6 = (bf16[2,112,768]{2,1,0:T(8,128)(2,1)S(1)}, bf16[2,112,768]{2,1,0:T(8,128)(2,1)}, u32[]{:S(2)}, u32[]{:S(2)}) collective-permute-start(bf16[2,112,768]{2,1,0:T(8,128)(2,1)S(1)} %get-tuple-element.94), channel_id=1, source_target_pairs={{0,8},{4,12},{8,0},{12,4},{1,9},{5,13},{9,1},{13,5},{2,10},{6,14},... | collective-permute-start | bytes 1032200 | tf_op jit(solution)/shard_map/ppermute | solution.py:201
  14.3 61.2 %collective-permute-start.7 = (bf16[2,112,768]{2,1,0:T(8,128)(2,1)S(1)}, bf16[2,112,768]{2,1,0:T(8,128)(2,1)}, u32[]{:S(2)}, u32[]{:S(2)}) collective-permute-start(bf16[2,112,768]{2,1,0:T(8,128)(2,1)S(1)} %get-tuple-element.94), channel_id=1, source_target_pairs={{0,12},{4,0},{8,4},{12,8},{1,13},{5,1},{9,5},{13,9},{2,14},{6,2},{... | collective-permute-start | bytes 1032200 | tf_op jit(solution)/shard_map/ppermute | solution.py:201
  15.9 5.4 collective-permute-start
  16.0 60.5 %collective-permute-start.1 = (bf16[768,576]{0,1:T(8,128)(2,1)}, bf16[768,576]{0,1:T(8,128)(2,1)}, u32[]{:S(2)}, u32[]{:S(2)}) collective-permute-start(bf16[768,576]{0,1:T(8,128)(2,1)} %bitcast.204), channel_id=1, source_target_pairs={{0,16},{16,0},{1,17},{17,1},{2,18},{18,2},{3,19},{19,3},{4,20},{20... | collective-permute-start | bytes 2654216 | tf_op jit(solution)/shard_map/ppermute | solution.py:17
  17.7 4.4 copy-start.73
  21.4 49.8 %collective-permute-start.2 = (bf16[192,768]{1,0:T(8,128)(2,1)S(1)}, bf16[192,768]{1,0:T(8,128)(2,1)}, u32[]{:S(2)}, u32[]{:S(2)}) collective-permute-start(bf16[192,768]{1,0:T(8,128)(2,1)S(1)} %bitcast.209), channel_id=1, source_target_pairs={{0,16},{16,0},{1,17},{17,1},{2,18},{18,2},{3,19},{19,3},{4,20},{20... | collective-permute-start | bytes 884744 | tf_op jit(solution)/shard_map/ppermute | solution.py:17
  71.1 97.0 %collective-permute-start.3 = (bf16[768,768]{1,0:T(8,128)(2,1)}, bf16[768,768]{1,0:T(8,128)(2,1)}, u32[]{:S(2)}, u32[]{:S(2)}) collective-permute-start(bf16[768,768]{1,0:T(8,128)(2,1)} %bitcast.202), channel_id=1, source_target_pairs={{0,16},{16,0},{1,17},{17,1},{2,18},{18,2},{3,19},{19,3},{4,20},{20... | collective-permute-start | bytes 3538952 | tf_op jit(solution)/shard_map/ppermute | solution.py:17
  73.0 107.0 %collective-permute-start.4 = (bf16[768,768]{1,0:T(8,128)(2,1)}, bf16[768,768]{1,0:T(8,128)(2,1)}, u32[]{:S(2)}, u32[]{:S(2)}) collective-permute-start(bf16[768,768]{1,0:T(8,128)(2,1)} %bitcast.12), channel_id=1, source_target_pairs={{0,16},{16,0},{1,17},{17,1},{2,18},{18,2},{3,19},{19,3},{4,20},{20... | collective-permute-start | bytes 3538952 | tf_op jit(solution)/shard_map/ppermute | solution.py:17
  81.5 5.6 copy-start.2
  81.6 18.1 %copy-start = (bf16[768,576]{1,0:T(8,128)(2,1)}, bf16[768,576]{1,0:T(8,128)(2,1)S(1)}, u32[]{:S(2)}) copy-start(bf16[768,576]{1,0:T(8,128)(2,1)S(1)} %get-tuple-element.101.refs_1_) | copy-start | bytes 2654212
  171.1 8.9 %copy-start.9 = (bf16[768,768]{1,0:T(8,128)(2,1)}, bf16[768,768]{1,0:T(8,128)(2,1)S(1)}, u32[]{:S(2)}) copy-start(bf16[768,768]{1,0:T(8,128)(2,1)S(1)} %get-tuple-element.100.refs_1_) | copy-start | bytes 3538948
  180.0 64.6 %copy-start.28 = (bf16[896,768]{1,0:T(8,128)(2,1)}, bf16[896,768]{1,0:T(8,128)(2,1)S(1)}, u32[]{:S(2)}) copy-start(bf16[896,768]{1,0:T(8,128)(2,1)S(1)} %get-tuple-element.97) | copy-start | bytes 4128772
  180.0 66.8 %copy-start.63 = (bf16[576,768]{1,0:T(8,128)(2,1)S(1)}, bf16[576,768]{1,0:T(8,128)(2,1)}, u32[]{:S(2)}) copy-start(bf16[576,768]{1,0:T(8,128)(2,1)} %copy.130) | copy-start | bytes 2654212
  325.7 9.9 %copy-start.23 = (bf16[2,4,112,768]{3,2,1,0:T(8,128)(2,1)}, bf16[2,4,112,768]{3,2,1,0:T(8,128)(2,1)S(1)}, u32[]{:S(2)}) copy-start(bf16[2,4,112,768]{3,2,1,0:T(8,128)(2,1)S(1)} %get-tuple-element.29) | copy-start | bytes 4128772
  325.8 9.9 %copy-start.50 = (bf16[2,4,112,768]{3,2,1,0:T(8,128)(2,1)S(1)}, bf16[2,4,112,768]{3,2,1,0:T(8,128)(2,1)}, u32[]{:S(2)}) copy-start(bf16[2,4,112,768]{3,2,1,0:T(8,128)(2,1)} %copy-done.49) | copy-start | bytes 4128772
  335.7 3.8 copy-start.11
  339.5 61.7 %copy-start.7 = (bf16[896,768]{1,0:T(8,128)(2,1)}, bf16[896,768]{1,0:T(8,128)(2,1)S(1)}, u32[]{:S(2)}) copy-start(bf16[896,768]{1,0:T(8,128)(2,1)S(1)} %get-tuple-element.152) | copy-start | bytes 4128772
  339.5 64.5 %copy-start.22 = (bf16[192,768]{1,0:T(8,128)(2,1)S(1)}, bf16[192,768]{1,0:T(8,128)(2,1)}, u32[]{:S(2)}) copy-start(bf16[192,768]{1,0:T(8,128)(2,1)} %get-tuple-element.108.refs_1_) | copy-start | bytes 884740
  409.9 4.2 copy-start.62
  415.8 3.6 copy-start.58
  421.9 7.5 copy-start.17
  431.9 62.7 %copy-start.29 = (bf16[896,768]{1,0:T(8,128)(2,1)S(1)}, bf16[896,768]{1,0:T(8,128)(2,1)}, u32[]{:S(2)}) copy-start(bf16[896,768]{1,0:T(8,128)(2,1)} %copy-done.28) | copy-start | bytes 4128772
  494.5 9.2 %copy-start.18 = (f32[2,112,768]{2,1,0:T(8,128)}, f32[2,112,768]{2,1,0:T(8,128)S(1)}, u32[]{:S(2)}) copy-start(f32[2,112,768]{2,1,0:T(8,128)S(1)} %get-tuple-element.34.refs_2_) | copy-start | bytes 2064388
  494.6 4.3 copy-start.83
  503.7 65.5 %copy-start.20 = (bf16[192,768]{1,0:T(8,128)(2,1)S(1)}, bf16[192,768]{1,0:T(8,128)(2,1)}, u32[]{:S(2)}) copy-start(bf16[192,768]{1,0:T(8,128)(2,1)} %get-tuple-element.109.refs_1_) | copy-start | bytes 884740
  576.9 4.2 copy-start.61
  584.2 4.4 copy-start.46
  584.2 6.7 copy-start.51
  584.2 6.7 copy-start.54
  590.9 3.4 copy-start.8
  590.9 3.4 copy-start.24
  590.9 3.4 copy-start.43
  594.3 3.4 copy-start.59
  594.3 91.3 %collective-permute-start.17 = (bf16[768,768]{1,0:T(8,128)(2,1)}, bf16[768,768]{1,0:T(8,128)(2,1)}, u32[]{:S(2)}, u32[]{:S(2)}) collective-permute-start(bf16[768,768]{1,0:T(8,128)(2,1)} %get-tuple-element.149), channel_id=1, source_target_pairs={{0,16},{16,0},{1,17},{17,1},{2,18},{18,2},{3,19},{19,3},{4,20},{20... | collective-permute-start | bytes 3538952 | tf_op jit(solution)/shard_map/ppermute | solution.py:17
  600.9 3.6 copy-start.55
  601.0 3.6 copy-start.56
  601.0 3.6 copy-start.65
  603.9 71.8 %collective-permute-start.15 = (bf16[192,768]{1,0:T(8,128)(2,1)}, bf16[192,768]{1,0:T(8,128)(2,1)}, u32[]{:S(2)}, u32[]{:S(2)}) collective-permute-start(bf16[192,768]{1,0:T(8,128)(2,1)} %get-tuple-element.145), channel_id=1, source_target_pairs={{0,16},{16,0},{1,17},{17,1},{2,18},{18,2},{3,19},{19,3},{4,20},{20... | collective-permute-start | bytes 884744 | tf_op jit(solution)/shard_map/ppermute | solution.py:17
  624.4 53.2 %collective-permute-start.13 = (bf16[768,576]{0,1:T(8,128)(2,1)}, bf16[768,576]{0,1:T(8,128)(2,1)}, u32[]{:S(2)}, u32[]{:S(2)}) collective-permute-start(bf16[768,576]{0,1:T(8,128)(2,1)} %copy.156), channel_id=1, source_target_pairs={{0,16},{16,0},{1,17},{17,1},{2,18},{18,2},{3,19},{19,3},{4,20},{20... | collective-permute-start | bytes 2654216 | tf_op jit(solution)/shard_map/ppermute | solution.py:17
  624.6 107.6 %collective-permute-start.14 = (bf16[1152]{0:T(1024)(128)(2,1)S(1)}, bf16[1152]{0:T(1024)(128)(2,1)S(1)}, u32[]{:S(2)}, u32[]{:S(2)}) collective-permute-start(bf16[1152]{0:T(1024)(128)(2,1)S(1)} %select_convert_fusion.4), channel_id=1, source_target_pairs={{0,16},{16,0},{1,17},{17,1},{2,18},{18,2},{3,19},{19,3},{4,20},{20... | collective-permute-start | bytes 6920 | tf_op jit(solution)/shard_map/ppermute | solution.py:17
  634.8 54.5 %collective-permute-start.16 = (bf16[768,768]{1,0:T(8,128)(2,1)}, bf16[768,768]{1,0:T(8,128)(2,1)}, u32[]{:S(2)}, u32[]{:S(2)}) collective-permute-start(bf16[768,768]{1,0:T(8,128)(2,1)} %get-tuple-element.147), channel_id=1, source_target_pairs={{0,16},{16,0},{1,17},{17,1},{2,18},{18,2},{3,19},{19,3},{4,20},{20... | collective-permute-start | bytes 3538952 | tf_op jit(solution)/shard_map/ppermute | solution.py:17
  636.1 39.6 %copy-start.52 = (f32[192,768]{1,0:T(8,128)S(1)}, f32[192,768]{1,0:T(8,128)}, u32[]{:S(2)}) copy-start(f32[192,768]{1,0:T(8,128)} %fusion.116) | copy-start | bytes 1769476
  685.6 3.6 copy-start.44
  685.6 3.6 copy-start.45
  691.9 7.1 copy-start.71
  691.9 7.1 copy-start.74
  691.9 7.1 copy-start.76
  691.9 7.7 copy-start.37
  691.9 36.7 %copy-start.33 = (f32[2,112,768]{2,1,0:T(8,128)S(1)}, f32[2,112,768]{2,1,0:T(8,128)}, u32[]{:S(2)}) copy-start(f32[2,112,768]{2,1,0:T(8,128)} %copy-done.32) | copy-start | bytes 2064388
  692.0 36.7 %copy-start.72 = (f32[768]{0:T(1024)S(1)}, f32[768]{0:T(1024)}, u32[]{:S(2)}) copy-start(f32[768]{0:T(1024)} %get-tuple-element.115) | copy-start | bytes 9220
  693.3 12.7 %collective-permute-start.10 = (bf16[2,112,768]{2,1,0:T(8,128)(2,1)S(1)}, bf16[2,112,768]{2,1,0:T(8,128)(2,1)S(1)}, u32[]{:S(2)}, u32[]{:S(2)}) collective-permute-start(bf16[2,112,768]{2,1,0:T(8,128)(2,1)S(1)} %get-tuple-element.104), channel_id=1, source_target_pairs={{0,12},{4,0},{8,4},{12,8},{1,13},{5,1},{9,5},{13,9},{2,14},{6,2},{... | collective-permute-start | bytes 1032200 | tf_op jit(solution)/shard_map/ppermute | solution.py:201
  697.5 16.5 %collective-permute-start.8 = (bf16[2,112,768]{2,1,0:T(8,128)(2,1)S(1)}, bf16[2,112,768]{2,1,0:T(8,128)(2,1)S(1)}, u32[]{:S(2)}, u32[]{:S(2)}) collective-permute-start(bf16[2,112,768]{2,1,0:T(8,128)(2,1)S(1)} %get-tuple-element.103), channel_id=1, source_target_pairs={{0,4},{4,8},{8,12},{12,0},{1,5},{5,9},{9,13},{13,1},{2,6},{6,10},{... | collective-permute-start | bytes 1032200 | tf_op jit(solution)/shard_map/ppermute | solution.py:201
  697.7 30.9 %collective-permute-start.9 = (bf16[2,112,768]{2,1,0:T(8,128)(2,1)S(1)}, bf16[2,112,768]{2,1,0:T(8,128)(2,1)S(1)}, u32[]{:S(2)}, u32[]{:S(2)}) collective-permute-start(bf16[2,112,768]{2,1,0:T(8,128)(2,1)S(1)} %get-tuple-element.105), channel_id=1, source_target_pairs={{0,8},{4,12},{8,0},{12,4},{1,9},{5,13},{9,1},{13,5},{2,10},{6,14},... | collective-permute-start | bytes 1032200 | tf_op jit(solution)/shard_map/ppermute | solution.py:201
  731.6 12.0 %collective-permute-start.12 = (f32[6,768]{1,0:T(8,128)S(1)}, f32[6,768]{1,0:T(8,128)S(1)}, u32[]{:S(2)}, u32[]{:S(2)}) collective-permute-start(f32[6,768]{1,0:T(8,128)S(1)} %broadcast_select_fusion.13), channel_id=1, source_target_pairs={{0,16},{16,0},{1,17},{17,1},{2,18},{18,2},{3,19},{19,3},{4,20},{20... | collective-permute-start | bytes 55304 | tf_op jit(solution)/shard_map/ppermute | solution.py:17
  731.7 87.1 %collective-permute-start.11 = (f32[2,112,768]{2,1,0:T(8,128)}, f32[2,112,768]{2,1,0:T(8,128)S(1)}, u32[]{:S(2)}, u32[]{:S(2)}) collective-permute-start(f32[2,112,768]{2,1,0:T(8,128)} %get-tuple-element.88), channel_id=1, source_target_pairs={{0,16},{16,0},{1,17},{17,1},{2,18},{18,2},{3,19},{19,3},{4,20},{20... | collective-permute-start | bytes 2064392 | tf_op jit(solution)/shard_map/ppermute | solution.py:17
  820.0 4.6 copy-start.64
  (39 other events, 70.5 us)
Sparse Core Ops, SparseCore 0:
  692.1 97.4 all-reduce.2

commit v2 on v1

--- a/solution.py
+++ b/solution.py
@@ -39,20 +39,22 @@
     return jax.nn.gelu(values, approximate=False)
 
 
-def greet(peers):
+def greet(peers, clip_peers=()):
     barrier = pltpu.get_barrier_semaphore()
     for peer in peers:
         pl.semaphore_signal(barrier, inc=1, device_id={"tensor": peer}, device_id_type=MESH)
-    pl.semaphore_wait(barrier, len(peers))
-
-
-def remote(src, dst, send_sem, recv_sem, peer):
+    for peer in clip_peers:
+        pl.semaphore_signal(barrier, inc=1, device_id={"dp": peer}, device_id_type=MESH)
+    pl.semaphore_wait(barrier, len(peers) + len(clip_peers))
+
+
+def remote(src, dst, send_sem, recv_sem, peer, axis="tensor"):
     return pltpu.make_async_remote_copy(
         src_ref=src,
         dst_ref=dst,
         send_sem=send_sem,
         recv_sem=recv_sem,
-        device_id={"tensor": peer},
+        device_id={axis: peer},
         device_id_type=MESH,
     )
 
@@ -80,7 +82,13 @@
         copy.wait()
 
 
-def exchange_kernel(group, transpose, mode, *refs):
+def exchange_kernel(group, transpose, mode, side, clip_group, *refs):
+    if side is not None:
+        *refs, side_send, side_recv = refs
+        at = {"backward": 5, "sum": 2}[mode]
+        side_in, refs = refs[at], refs[:at] + refs[at + 1 :]
+        at = {"backward": 8, "sum": 3}[mode]
+        side_out, refs = refs[at], refs[:at] + refs[at + 1 :]
     if mode == "forward":
         act, weight, resid, bias, gain, shift, value_out, full_out, *scratch = refs
     elif mode == "backward":
@@ -98,7 +106,18 @@
     def product(c, j):
         return lax.dot_general(act[c, j], weight[...], contract, preferred_element_type=f32)
 
-    greet(peers)
+    here = lax.axis_index("dp")
+    clip_peers = [] if side is None else [lax.rem(here + k, clip_group) for k in range(1, clip_group)]
+    greet(peers, clip_peers)
+    side_copies = []
+    for k, peer in enumerate(clip_peers):
+        source = side_in.at[peer] if side == "scatter" else side_in
+        target = side_out.at[k] if side == "scatter" else side_out.at[here]
+        copy = remote(source, target, side_send.at[k], side_recv.at[k], peer, "dp")
+        copy.start()
+        side_copies.append(copy)
+    if side == "gather":
+        side_out[here] = side_in[...]
     copies = {}
     for c in range(clips):
         for k, peer in enumerate(peers):
@@ -133,7 +152,7 @@
             copy.start()
             waits.append(copy)
         full_out[c, me] = own[c]
-    for copy in waits:
+    for copy in waits + side_copies:
         copy.wait()
 
 
@@ -166,7 +185,7 @@
     return full.reshape(clips * group * share, width)
 
 
-def exchange(mode, number, act, weight, transpose, share, *rest):
+def exchange(mode, number, act, weight, transpose, share, *rest, side=None, parcel=None):
     group = lax.axis_size("tensor")
     width = weight.shape[0] if transpose else weight.shape[1]
     depth = act.shape[-1]
@@ -182,8 +201,14 @@
         scratch = scratch + [pltpu.VMEM((clips, share, width), bf16)] + sems
     scratch = scratch + sems
     rest = tuple(item[None] if item.ndim == 1 else item for item in rest)
+    clip_group = lax.axis_size("dp")
+    if side is not None:
+        rest = rest + (parcel,)
+        count = clip_group - 1 if side == "scatter" else clip_group
+        outs = outs + (jax.ShapeDtypeStruct((count,) + parcel.shape[-2:], bf16),)
+        scratch = scratch + [DMA((clip_group - 1,)), DMA((clip_group - 1,))]
     got = pl.pallas_call(
-        functools.partial(exchange_kernel, group, transpose, mode),
+        functools.partial(exchange_kernel, group, transpose, mode, side, clip_group),
         out_shape=outs,
         in_specs=[VMEM] * (2 + len(rest)),
         out_specs=tuple(VMEM for _ in outs),
@@ -192,8 +217,17 @@
         name=mode + "_exchange",
     )(act, weight, *rest)
     if mode == "sum":
-        return got[0]
-    return got[:-1] + (got[-1].reshape(clips * group * share, width),)
+        return got
+    at = len(outs) - 1 if side is None else len(outs) - 2
+    return got[:at] + (got[at].reshape(clips * group * share, width),) + got[at + 1 :]
+
+
+def pack_half(grads, upper):
+    parts = []
+    for grad in grads:
+        rows = grad.shape[0] // 2
+        parts.append(lax.dynamic_slice_in_dim(grad, upper * rows, rows, 0))
+    return jnp.concatenate(parts)
 
 
 def shifted(block, distance):
@@ -316,9 +350,18 @@
         pre_grad = jax.vjp(exact_gelu, pre)[1](active_grad)[0].astype(bf16)
         up_bias_grad = jnp.sum(pre_grad.astype(f32), axis=0)
         up_grad = jnp.einsum("nd,nf->df", gathered_two[l], pre_grad, preferred_element_type=f32)
-        sum_two, middle_grad, full = exchange(
-            "backward", 3, pre_grad, up[l], True, share, incoming, middles[l], gain[1]
-        )
+        if l == 1:
+            sum_two, middle_grad, full = exchange(
+                "backward", 3, pre_grad, up[l], True, share, incoming, middles[l], gain[1]
+            )
+        else:
+            sum_two, middle_grad, full, landed = exchange(
+                "backward", 6, pre_grad, up[l], True, share, incoming, middles[l], gain[1],
+                side="scatter", parcel=parcel,
+            )
+            total = lax.dynamic_index_in_dim(parcel, lax.axis_index("dp"), 0, keepdims=False)
+            total = total.astype(f32) + jnp.sum(landed.astype(f32), axis=0)
+            reduced_part = total.astype(bf16)
         normed_two = norm_stats(middles[l])[0]
         queries, keys, values, prob, prob_low, attended = attn[l]
         out_grad = jnp.einsum("nc,nd->cd", attended, full, preferred_element_type=f32)
@@ -346,14 +389,18 @@
                 jnp.sum(values_grad.astype(f32), axis=(0, 1)),
             ]
         )
-        qkv_grad = jnp.einsum("nd,nc->dc", gathered[l], flat, preferred_element_type=f32)
+        qkv_grad = jnp.einsum("nd,nc->cd", gathered[l], flat, preferred_element_type=f32)
         end_grads = [jnp.sum(middle_grad, axis=(0, 1)), jnp.sum(incoming, axis=(0, 1))]
         if l == 1:
             sum_one, entry_grad, grads_full = exchange(
                 "backward", 4, flat, qkv[l], True, share, middle_grad, entries[l], gain[0]
             )
         else:
-            sum_one = exchange("sum", 5, flat, qkv[l], True, share)
+            flat, result = lax.optimization_barrier((flat, result))
+            sum_one, top_half = exchange(
+                "sum", 5, flat, qkv[l], True, share, side="gather", parcel=reduced_part
+            )
+            top_half = top_half.reshape(-1, width)
             entry_grad = middle_grad + norm_back(sum_one, entries[l], gain[0])
         normed_one = norm_stats(entries[l])[0]
         shared[l] = jnp.stack(
@@ -365,13 +412,12 @@
             ]
             + end_grads
         )
-        layer_grads[l] = (
-            qkv_grad,
-            out_grad,
-            up_grad,
-            down_grad,
-            jnp.concatenate([bias_grad.reshape(-1), up_bias_grad]),
-        )
+        layer_grads[l] = jnp.concatenate([bias_grad.reshape(-1), up_bias_grad])
+        grads = (qkv_grad, out_grad, up_grad, down_grad)
+        given = swap_pipe(pack_half(grads, 1 - section).astype(bf16))
+        half_sum = (pack_half(grads, section) + given.astype(f32)).astype(bf16)
+        if l == 1:
+            parcel = half_sum.reshape(lax.axis_size("dp"), -1, width)
         incoming = entry_grad
 
     def reduced(first, second):
@@ -379,9 +425,17 @@
         other = jnp.where(leading, second, first)
         return mine + swap_pipe(other.astype(bf16)).astype(f32)
 
-    summed = [
-        lax.psum(reduced(a, b).astype(bf16), "dp").astype(f32) for a, b in zip(*layer_grads)
-    ]
+    first_half = lax.psum(half_sum, "dp")
+    kept = jnp.where(leading, first_half, top_half)
+    other = swap_pipe(jnp.where(leading, top_half, first_half))
+    lower = jnp.where(leading, kept, other)
+    upper = jnp.where(leading, other, kept)
+    summed, at = [], 0
+    for grad in grads:
+        rows = grad.shape[0] // 2
+        summed.append(jnp.concatenate([lower[at : at + rows], upper[at : at + rows]]).astype(f32))
+        at += rows
+    vectors = lax.psum(reduced(*layer_grads), "dp")
     common = jnp.where(leading, shared[0], shared[1]) + swap_pipe(
         jnp.where(leading, shared[1], shared[0])
     )
@@ -397,12 +451,12 @@
         boundary[None],
         common[None, 0:2],
         common[None, 2:4],
-        summed[0].reshape(1, width, heads, 3 * hdim),
-        summed[4][:bias_size].reshape(1, 2, heads, hdim),
+        summed[0].T.reshape(1, width, heads, 3 * hdim),
+        vectors[:bias_size].reshape(1, 2, heads, hdim),
         summed[1].reshape(1, heads, hdim, width),
         common[None, 4:6],
         summed[2][None],
-        summed[4][bias_size:][None],
+        vectors[bias_size:][None],
         summed[3][None],
     )
 

time: 844 us -> 831 us (0.985)
  matrix products: 99.6 us -> 88.5 us
    broadcast_in_dim x4 -> x0, other arithmetic: 10.9 us -> none  [the longest x2 5.67 us: per_device(): summed[2][None]]
    ppermute x6, waiting for transfers between devices: 28.8 us -> 20 us  [shifted(): lax.ppermute(block, 'tensor', [(i, (i + distance) % size) for i in range(...]
    another operation x8 -> x6, local copies, waits for them, and re-layouts: 20.6 us -> 13.3 us  [exchange(): act = act.reshape(-1, group, share, depth)]
    unnamed x174 -> x192, local copies, waits for them, and re-layouts: 22.8 us -> 26 us
  transfers between devices with their start and end apart: 19 -> 18, of which waited for: 3 -> 4; matrix products, arithmetic and copies ran while one was open for 14% -> 10% of each run, Pallas kernels for 17% -> 17%
where the time goes in v2:
time: 831 us; the launch traced here: 821 us
  Pallas kernels  458 us (55%)
  local copies, waits for them, and re-layouts  89.5 us (11%)
  matrix products  88.5 us (11%)
  blocking collectives  84.7 us (10%)
  other arithmetic  39.8 us (5%)
  waiting for transfers between devices  27.5 us (3%)
  starting transfers between devices  17.3 us (2%)
  between operations  15.7 us (2%)
    pallas_call x7, Pallas kernels, exchange(): pl.pallas_call(functools.partial(exchange_kernel, group, transpose, mode,...  411 us
    psum x1, blocking collectives, per_device(): common = lax.psum(common, ('tensor', 'dp'))  75.6 us
    pallas_call x1, Pallas kernels, gather_normed(): pl.pallas_call(functools.partial(gather_kernel, group), out_shape=jax.Sha...  47.3 us
    unnamed x192, local copies, waits for them, and re-layouts  26 us
    ppermute x6, waiting for transfers between devices, shifted(): lax.ppermute(block, 'tensor', [(i, (i + distance) % size) for i in range(...  20 us
    dot_general x2, matrix products, per_device(): pre = jnp.dot(full, up[l], preferred_element_type=f32) + up_vector  18.6 us
  transfers between devices with their start and end apart: 18, of which 4 were waited for; matrix products, arithmetic and copies ran while one was open for 10% of the time, Pallas kernels for 17%

profile of v2, /device:TPU:0, one launch (start us, length us, event | category | flops | bytes accessed | tf_op | source)
XLA Modules:
  0.0 821.4 jit_solution(6643769529936528534)
XLA Ops:
  10.7 4.0 collective-permute-start.6
  14.7 1.6 collective-permute-start.5
  16.3 2.2 collective-permute-start.7
  20.3 2.2 copy.72
  24.3 47.3 %gather_normed.1 = bf16[2,4,112,768]{3,2,1,0:T(8,128)(2,1)S(1)} custom-call(f32[2,112,768]{2,1,0:T(8,128)S(1)} %get-tuple-element.87.value_ref.refs_2_, f32[1,768]{1,0:T(1,128)S(1)} %slice.236.gain_ref, f32[1,768]{1,0:T(1,128)S(1)} %slice.238.shift_ref), custom_call_target="tpu_custom_call" | custom-call | tf_op jit(solution)/shard_map/gather_normed/pallas_call | solution.py:172
  71.8 2.3 broadcast_select_fusion.13
  74.2 1.7 bitcast_dynamic-update-slice_fusion.2
  75.9 1.7 bitcast_dynamic-update-slice_fusion.1
  77.6 1.8 bitcast_dynamic-update-slice_fusion
  79.4 2.2 copy.73
  81.6 1.7 broadcast_select_fusion.6
  84.8 4.1 fusion.113
  88.9 5.7 fusion.103
  94.6 3.5 fusion.57
  99.2 2.0 reshape_reshape.9
  104.8 63.7 %forward_exchange.3 = (f32[2,112,768]{2,1,0:T(8,128)S(1)}, bf16[2,4,112,768]{3,2,1,0:T(8,128)(2,1)S(1)}) custom-call(bf16[2,4,112,192]{3,2,1,0:T(8,128)(2,1)S(1)} %copy.76.refs_0_, bf16[192,768]{1,0:T(8,128)(2,1)S(1)} %copy-done.21, f32[2,112,768]{2,1,0:T(8,128)S(1)} %get-tuple-element.87.value_ref.refs_2_, f32[1,768]{1,0:T(1,128)S(1)} %slice.247.refs_3_, ...), custom_call_target="tpu_custom_call" | custom-call | tf_op jit(solution)/shard_map/forward_exchange/pallas_call | solution.py:210
  169.9 2.9 broadcast_select_fusion.3
  172.8 8.9 %multiply_convert_fusion.3 = (bf16[896,768]{1,0:T(8,128)(2,1)S(1)}, f32[896,768]{1,0:T(8,128)}, f32[896,768]{1,0:T(8,128)}) fusion(f32[768]{0:T(1024)S(1)} %get-tuple-element.126, bf16[896,768]{1,0:T(8,128)(2,1)S(1)} %bitcast.204, bf16[768,768]{1,0:T(8,128)(2,1)S(1)} %get-tuple-element.97.refs_1_), kind=kOutput, calls=%fused_computation.38 | convolution fusion | flops 1102381056 | bytes 9440256 | tf_op jit(solution)/shard_map/dot_general | solution.py:329
  181.9 64.1 %forward_exchange.4 = (f32[2,112,768]{2,1,0:T(8,128)S(1)}, bf16[2,4,112,768]{3,2,1,0:T(8,128)(2,1)S(1)}) custom-call(bf16[2,4,112,768]{3,2,1,0:T(8,128)(2,1)S(1)} %bitcast.201, bf16[768,768]{1,0:T(8,128)(2,1)S(1)} %broadcast_select_fusion.4.refs_1_, f32[2,112,768]{2,1,0:T(8,128)S(1)} %get-tuple-element.31.refs_2_.refs_3_, f32[1,768]{1,0:T(1,128)S(1)} %slice.254.refs_3_, ...), custom_call_target="tpu_custom_call" | custom-call | tf_op jit(solution)/shard_map/forward_exchange/pallas_call | solution.py:210
  248.2 2.5 fusion.114
  250.7 5.7 fusion.104
  256.4 3.5 fusion.51
  262.1 2.0 copy.81.refs_0_
  266.0 63.2 %forward_exchange.5 = (f32[2,112,768]{2,1,0:T(8,128)S(1)}, bf16[2,4,112,768]{3,2,1,0:T(8,128)(2,1)S(1)}) custom-call(bf16[2,4,112,192]{3,2,1,0:T(8,128)(2,1)S(1)} %copy-done.25, bf16[192,768]{1,0:T(8,128)(2,1)S(1)} %copy-done.23, f32[2,112,768]{2,1,0:T(8,128)S(1)} %get-tuple-element.33.refs_2_.refs_3_, f32[1,768]{1,0:T(1,128)S(1)} %slice.267.refs_3_, ...), custom_call_target="tpu_custom_call" | custom-call | tf_op jit(solution)/shard_map/forward_exchange/pallas_call | solution.py:210
  329.3 9.7 %multiply_convert_fusion.2 = (bf16[896,768]{1,0:T(8,128)(2,1)}, f32[896,768]{1,0:T(8,128)S(1)}, f32[896,768]{1,0:T(8,128)S(1)}) fusion(f32[768]{0:T(1024)S(1)} %get-tuple-element.117, bf16[896,768]{1,0:T(8,128)(2,1)S(1)} %bitcast.210, bf16[768,768]{1,0:T(8,128)(2,1)} %get-tuple-element.96.refs_1_), kind=kOutput, calls=%fused_computation.22 | convolution fusion | flops 1102381056 | bytes 9440256 | tf_op jit(solution)/shard_map/dot_general | solution.py:329
  339.0 3.8 convert_reduce_fusion
  342.9 2.9 fusion.117
  345.8 63.1 %backward_exchange.3 = (f32[2,112,768]{2,1,0:T(8,128)S(1)}, f32[2,112,768]{2,1,0:T(8,128)S(1)}, bf16[2,4,112,768]{3,2,1,0:T(8,128)(2,1)S(1)}) custom-call(bf16[2,4,112,768]{3,2,1,0:T(8,128)(2,1)S(1)} %bitcast.203, bf16[768,768]{1,0:T(8,128)(2,1)S(1)} %copy-done.11, f32[2,112,768]{2,1,0:T(8,128)S(1)} %get-tuple-element.83.refs_2_, ...), custom_call_target="tpu_custom_call" | custom-call | tf_op jit(solution)/shard_map/backward_exchange/pallas_call | solution.py:210
  413.4 3.8 convert_reduce_fusion.3
  417.3 3.8 multiply_reduce_fusion.1
  421.1 1.6 multiply_convert_fusion.1
  425.5 2.4 copy.92
  427.9 3.8 reshape_reshape.11
  432.8 3.3 fusion.118
  436.1 1.6 fusion.116
  438.6 2.2 dynamic-slice_convert_fusion.3
  440.9 3.9 reshape.413
  444.8 3.3 copy.91.refs_0_
  450.5 62.7 %backward_exchange.4 = (f32[2,112,768]{2,1,0:T(8,128)S(1)}, f32[2,112,768]{2,1,0:T(8,128)S(1)}, bf16[2,4,112,768]{3,2,1,0:T(8,128)(2,1)S(1)}) custom-call(bf16[2,4,112,576]{3,2,1,0:T(8,128)(2,1)S(1)} %copy-done.15, bf16[768,576]{1,0:T(8,128)(2,1)S(1)} %copy-done.4, f32[2,112,768]{2,1,0:T(8,128)S(1)} %copy-done.19, ...), custom_call_target="tpu_custom_call" | custom-call | tf_op jit(solution)/shard_map/backward_exchange/pallas_call | solution.py:210
  519.4 2.0 convert_reduce_fusion.1
  527.6 62.4 %backward_exchange.5 = (f32[2,112,768]{2,1,0:T(8,128)S(1)}, f32[2,112,768]{2,1,0:T(8,128)S(1)}, bf16[2,4,112,768]{3,2,1,0:T(8,128)(2,1)S(1)}, bf16[3,288,768]{2,1,0:T(8,128)(2,1)S(1)}) custom-call(bf16[2,4,112,768]{3,2,1,0:T(8,128)(2,1)S(1)} %bitcast.202, bf16[768,768]{1,0:T(8,128)(2,1)S(1)} %copy-done.10, f32[2,112,768]{2,1,0:T(8,128)S(1)} %get-tuple-element.39.refs_2_, ...), custom_call_target="tpu_custom_call" | custom-call | tf_op jit(solution)/shard_map/backward_exchange/pallas_call | solution.py:210
  595.3 2.1 reshape.418
  597.4 3.8 convert_reduce_fusion.5
  601.2 3.8 multiply_reduce_fusion
  605.1 1.6 multiply_convert_fusion
  610.5 2.2 copy.99
  612.8 3.9 reshape.419
  616.6 2.8 fusion.119
  623.0 3.6 convolution_convert_fusion
  628.1 2.2 dynamic-slice_bitcast_fusion.2
  630.3 3.8 collective-permute-start.9
  634.1 2.2 collective-permute-start.11
  640.3 3.2 fusion.9
  645.5 4.9 collective-permute-done.11
  650.4 14.8 %collective-permute-done.10 = bf16[2,112,768]{2,1,0:T(8,128)(2,1)} collective-permute-done((bf16[2,112,768]{2,1,0:T(8,128)(2,1)}, bf16[2,112,768]{2,1,0:T(8,128)(2,1)}, u32[]{:S(2)}, u32[]{:S(2)}) %collective-permute-start.10) | collective-permute-done | bytes 344096 | tf_op jit(solution)/shard_map/ppermute | solution.py:235
  665.2 2.5 fusion.93
  668.1 2.4 copy.101
  672.0 31.6 %sum_exchange.1 = (f32[2,112,768]{2,1,0:T(8,128)S(1)}, bf16[4,288,768]{2,1,0:T(8,128)(2,1)S(1)}) custom-call(bf16[2,4,112,576]{3,2,1,0:T(8,128)(2,1)S(1)} %bitcast.198, bf16[768,576]{1,0:T(8,128)(2,1)S(1)} %copy-done.2, bf16[288,768]{1,0:T(8,128)(2,1)S(1)} %fusion.64.refs_2_), custom_call_target="tpu_custom_call" | custom-call | tf_op jit(solution)/shard_map/sum_exchange/pallas_call | solution.py:210
  704.9 7.4 all-reduce.2.cloned.1.call-done
  717.2 9.1 %psum.23 = f32[1152]{0:T(1024)S(1)} all-reduce(f32[1152]{0:T(1024)S(1)} %convert_add_fusion.2), channel_id=1, replica_groups=mesh['pipe'=2,'tensor'=4,'dp'=4] {'dp'}, use_global_device_ids=true, to_apply=%region_37.38 | all-reduce | flops 1152 | bytes 9216 | tf_op jit(solution)/shard_map/psum | solution.py:438
  727.6 75.6 %psum.21 = f32[6,768]{1,0:T(8,128)S(1)} all-reduce(f32[6,768]{1,0:T(8,128)S(1)} %select_add_fusion), channel_id=1, replica_groups=mesh['pipe'=2,'tensor'=4,'dp'=4] {'tensor','dp'}, use_global_device_ids=true, to_apply=%region_29.30 | all-reduce | flops 4608 | bytes 36864 | tf_op jit(solution)/shard_map/psum | solution.py:442
  803.8 2.5 maximum_select_fusion
  806.3 2.3 broadcast_select_fusion.1
  811.2 1.6 maximum_convert_fusion.1
  (356 shorter events, 78.7 us)
Async XLA Ops:
  7.2 11.3 %copy-start.84 = (f32[1,2,3,64]{3,1,2,0:T(2,128)S(1)}, f32[1,2,3,64]{3,1,2,0:T(2,128)}, u32[]{:S(2)}) copy-start(f32[1,2,3,64]{3,1,2,0:T(2,128)} %param.16) | copy-start | bytes 4612
  7.2 11.4 %copy-start.81 = (f32[1,2,768]{2,1,0:T(2,128)S(1)}, f32[1,2,768]{2,1,0:T(2,128)}, u32[]{:S(2)}) copy-start(f32[1,2,768]{2,1,0:T(2,128)} %param.13) | copy-start | bytes 18436
  7.2 11.4 %copy-start.82 = (f32[1,2,768]{2,1,0:T(2,128)S(1)}, f32[1,2,768]{2,1,0:T(2,128)}, u32[]{:S(2)}) copy-start(f32[1,2,768]{2,1,0:T(2,128)} %param.14) | copy-start | bytes 18436
  7.2 11.4 %copy-start.83 = (f32[1,2,768]{2,1,0:T(2,128)S(1)}, f32[1,2,768]{2,1,0:T(2,128)}, u32[]{:S(2)}) copy-start(f32[1,2,768]{2,1,0:T(2,128)} %param.18) | copy-start | bytes 18436
  7.2 11.4 %copy-start.85 = (f32[1,768]{1,0:T(1,128)S(1)}, f32[1,768]{1,0:T(1,128)}, u32[]{:S(2)}) copy-start(f32[1,768]{1,0:T(1,128)} %param.20) | copy-start | bytes 9220
  7.2 12.1 %copy-start.73 = (f32[4,112,768]{2,1,0:T(8,128)S(1)}, f32[4,112,768]{2,1,0:T(8,128)}, u32[]{:S(2)}) copy-start(f32[4,112,768]{2,1,0:T(8,128)} %param.11) | copy-start | bytes 4128772
  7.2 705.1 %all-reduce.2.cloned.1.call-start = ((), (), s32[]{:S(2)}) async-start(), calls=%async_computation | async-start | bytes 3538944 | tf_op jit(solution)/shard_map/psum | solution.py:428
  10.7 65.2 %collective-permute-start.6 = (bf16[2,112,768]{2,1,0:T(8,128)(2,1)S(1)}, bf16[2,112,768]{2,1,0:T(8,128)(2,1)}, u32[]{:S(2)}, u32[]{:S(2)}) collective-permute-start(bf16[2,112,768]{2,1,0:T(8,128)(2,1)S(1)} %get-tuple-element.91), channel_id=1, source_target_pairs={{0,8},{4,12},{8,0},{12,4},{1,9},{5,13},{9,1},{13,5},{2,10},{6,14},... | collective-permute-start | bytes 1032200 | tf_op jit(solution)/shard_map/ppermute | solution.py:235
  14.7 59.4 %collective-permute-start.5 = (bf16[2,112,768]{2,1,0:T(8,128)(2,1)S(1)}, bf16[2,112,768]{2,1,0:T(8,128)(2,1)}, u32[]{:S(2)}, u32[]{:S(2)}) collective-permute-start(bf16[2,112,768]{2,1,0:T(8,128)(2,1)S(1)} %get-tuple-element.91), channel_id=1, source_target_pairs={{0,4},{4,8},{8,12},{12,0},{1,5},{5,9},{9,13},{13,1},{2,6},{6,10},{... | collective-permute-start | bytes 1032200 | tf_op jit(solution)/shard_map/ppermute | solution.py:235
  16.3 61.4 %collective-permute-start.7 = (bf16[2,112,768]{2,1,0:T(8,128)(2,1)S(1)}, bf16[2,112,768]{2,1,0:T(8,128)(2,1)}, u32[]{:S(2)}, u32[]{:S(2)}) collective-permute-start(bf16[2,112,768]{2,1,0:T(8,128)(2,1)S(1)} %get-tuple-element.91), channel_id=1, source_target_pairs={{0,12},{4,0},{8,4},{12,8},{1,13},{5,1},{9,5},{13,9},{2,14},{6,2},{... | collective-permute-start | bytes 1032200 | tf_op jit(solution)/shard_map/ppermute | solution.py:235
  18.8 4.3 collective-permute-start
  18.8 60.5 %collective-permute-start.1 = (bf16[768,576]{0,1:T(8,128)(2,1)}, bf16[768,576]{0,1:T(8,128)(2,1)}, u32[]{:S(2)}, u32[]{:S(2)}) collective-permute-start(bf16[768,576]{0,1:T(8,128)(2,1)} %bitcast.3), channel_id=1, source_target_pairs={{0,16},{16,0},{1,17},{17,1},{2,18},{18,2},{3,19},{19,3},{4,20},{20... | collective-permute-start | bytes 2654216 | tf_op jit(solution)/shard_map/ppermute | solution.py:17
  19.5 3.6 copy-start.77
  23.1 48.6 %collective-permute-start.2 = (bf16[192,768]{1,0:T(8,128)(2,1)}, bf16[192,768]{1,0:T(8,128)(2,1)}, u32[]{:S(2)}, u32[]{:S(2)}) collective-permute-start(bf16[192,768]{1,0:T(8,128)(2,1)} %bitcast.8), channel_id=1, source_target_pairs={{0,16},{16,0},{1,17},{17,1},{2,18},{18,2},{3,19},{19,3},{4,20},{20... | collective-permute-start | bytes 884744 | tf_op jit(solution)/shard_map/ppermute | solution.py:17
  71.6 7.7 copy-start.26
  71.7 110.1 %collective-permute-start.4 = (bf16[768,768]{1,0:T(8,128)(2,1)}, bf16[768,768]{1,0:T(8,128)(2,1)}, u32[]{:S(2)}, u32[]{:S(2)}) collective-permute-start(bf16[768,768]{1,0:T(8,128)(2,1)} %bitcast.223), channel_id=1, source_target_pairs={{0,16},{16,0},{1,17},{17,1},{2,18},{18,2},{3,19},{19,3},{4,20},{20... | collective-permute-start | bytes 3538952 | tf_op jit(solution)/shard_map/ppermute | solution.py:17
  74.1 95.8 %collective-permute-start.3 = (bf16[768,768]{1,0:T(8,128)(2,1)}, bf16[768,768]{1,0:T(8,128)(2,1)}, u32[]{:S(2)}, u32[]{:S(2)}) collective-permute-start(bf16[768,768]{1,0:T(8,128)(2,1)} %bitcast.221), channel_id=1, source_target_pairs={{0,16},{16,0},{1,17},{17,1},{2,18},{18,2},{3,19},{19,3},{4,20},{20... | collective-permute-start | bytes 3538952 | tf_op jit(solution)/shard_map/ppermute | solution.py:17
  83.3 5.6 copy-start.1
  83.3 17.9 %copy-start.3 = (bf16[768,576]{1,0:T(8,128)(2,1)}, bf16[768,576]{1,0:T(8,128)(2,1)S(1)}, u32[]{:S(2)}) copy-start(bf16[768,576]{1,0:T(8,128)(2,1)S(1)} %get-tuple-element.98.refs_1_) | copy-start | bytes 2654212
  98.8 5.9 copy-start.21
  172.8 8.9 %copy-start.9 = (bf16[768,768]{1,0:T(8,128)(2,1)}, bf16[768,768]{1,0:T(8,128)(2,1)S(1)}, u32[]{:S(2)}) copy-start(bf16[768,768]{1,0:T(8,128)(2,1)S(1)} %get-tuple-element.97.refs_1_) | copy-start | bytes 3538948
  172.8 8.9 %copy-start.61 = (bf16[1,768,768]{2,1,0:T(8,128)(2,1)S(1)}, bf16[1,768,768]{2,1,0:T(8,128)(2,1)}, u32[]{:S(2)}) copy-start(bf16[1,768,768]{2,1,0:T(8,128)(2,1)} %param.21) | copy-start | bytes 3538948
  181.7 64.3 %copy-start.27 = (bf16[896,768]{1,0:T(8,128)(2,1)}, bf16[896,768]{1,0:T(8,128)(2,1)S(1)}, u32[]{:S(2)}) copy-start(bf16[896,768]{1,0:T(8,128)(2,1)S(1)} %get-tuple-element.92) | copy-start | bytes 4128772
  181.7 66.5 %copy-start.69 = (bf16[576,768]{1,0:T(8,128)(2,1)S(1)}, bf16[576,768]{1,0:T(8,128)(2,1)}, u32[]{:S(2)}) copy-start(bf16[576,768]{1,0:T(8,128)(2,1)} %copy.79) | copy-start | bytes 2654212
  329.3 9.7 %copy-start.62 = (bf16[1,768,768]{2,1,0:T(8,128)(2,1)S(1)}, bf16[1,768,768]{2,1,0:T(8,128)(2,1)}, u32[]{:S(2)}) copy-start(bf16[1,768,768]{2,1,0:T(8,128)(2,1)} %param.21) | copy-start | bytes 3538948
  345.8 65.9 %copy-start.24 = (bf16[192,768]{1,0:T(8,128)(2,1)S(1)}, bf16[192,768]{1,0:T(8,128)(2,1)}, u32[]{:S(2)}) copy-start(bf16[192,768]{1,0:T(8,128)(2,1)} %get-tuple-element.109.refs_1_) | copy-start | bytes 884740
  413.4 3.8 copy-start.65
  413.4 3.8 copy-start.71
  413.4 7.7 slice-start.2
  417.3 3.8 slice-start.3
  425.5 6.2 copy-start.52
  438.6 9.4 %copy-start.19 = (f32[2,112,768]{2,1,0:T(8,128)S(1)}, f32[2,112,768]{2,1,0:T(8,128)}, u32[]{:S(2)}) copy-start(f32[2,112,768]{2,1,0:T(8,128)} %copy-done.18) | copy-start | bytes 2064388
  450.5 62.8 %copy-start.28 = (bf16[896,768]{1,0:T(8,128)(2,1)S(1)}, bf16[896,768]{1,0:T(8,128)(2,1)}, u32[]{:S(2)}) copy-start(bf16[896,768]{1,0:T(8,128)(2,1)} %copy-done.27) | copy-start | bytes 4128772
  513.3 3.5 copy-start.37
  513.3 13.5 %copy-start.20 = (f32[2,112,768]{2,1,0:T(8,128)}, f32[2,112,768]{2,1,0:T(8,128)S(1)}, u32[]{:S(2)}) copy-start(f32[2,112,768]{2,1,0:T(8,128)S(1)} %get-tuple-element.39.refs_2_) | copy-start | bytes 2064388
  517.0 9.4 %collective-permute-start.8 = (bf16[1152,768]{1,0:T(8,128)(2,1)S(1)}, bf16[1152,768]{1,0:T(8,128)(2,1)S(1)}, u32[]{:S(2)}, u32[]{:S(2)}) collective-permute-start(bf16[1152,768]{1,0:T(8,128)(2,1)S(1)} %pad_maximum_fusion), channel_id=1, source_target_pairs={{0,16},{16,0},{1,17},{17,1},{2,18},{18,2},{3,19},{19,3},{4,20},{20... | collective-permute-start | bytes 5308424 | tf_op jit(solution)/shard_map/ppermute | solution.py:17
  521.4 3.9 copy-start.60
  526.8 63.3 %copy-start = (bf16[1152,768]{1,0:T(8,128)(2,1)}, bf16[1152,768]{1,0:T(8,128)(2,1)S(1)}, u32[]{:S(2)}) copy-start(bf16[1152,768]{1,0:T(8,128)(2,1)S(1)} %fusion.8) | copy-start | bytes 5308420
  527.6 66.3 %copy-start.22 = (bf16[192,768]{1,0:T(8,128)(2,1)S(1)}, bf16[192,768]{1,0:T(8,128)(2,1)}, u32[]{:S(2)}) copy-start(bf16[192,768]{1,0:T(8,128)(2,1)} %get-tuple-element.110.refs_1_) | copy-start | bytes 884740
  597.4 3.8 copy-start.64
  597.4 3.8 copy-start.72
  597.4 7.7 slice-start
  601.2 3.8 slice-start.1
  616.6 4.1 copy-start.45
  616.6 4.1 copy-start.46
  616.6 4.1 copy-start.70
  622.1 18.2 %collective-permute-start.14 = (bf16[1152,768]{1,0:T(8,128)(2,1)}, bf16[1152,768]{1,0:T(8,128)(2,1)}, u32[]{:S(2)}, u32[]{:S(2)}) collective-permute-start(bf16[1152,768]{1,0:T(8,128)(2,1)} %pad_maximum_fusion.1), channel_id=1, source_target_pairs={{0,16},{16,0},{1,17},{17,1},{2,18},{18,2},{3,19},{19,3},{4,20},{20... | collective-permute-start | bytes 5308424 | tf_op jit(solution)/shard_map/ppermute | solution.py:17
  630.3 9.8 %copy-start.50 = (f32[192,768]{1,0:T(8,128)S(1)}, f32[192,768]{1,0:T(8,128)}, u32[]{:S(2)}) copy-start(f32[192,768]{1,0:T(8,128)} %copy-done.49) | copy-start | bytes 1769476
  630.3 15.1 %collective-permute-start.9 = (bf16[2,112,768]{2,1,0:T(8,128)(2,1)}, bf16[2,112,768]{2,1,0:T(8,128)(2,1)}, u32[]{:S(2)}, u32[]{:S(2)}) collective-permute-start(bf16[2,112,768]{2,1,0:T(8,128)(2,1)} %get-tuple-element.104), channel_id=1, source_target_pairs={{0,4},{4,8},{8,12},{12,0},{1,5},{5,9},{9,13},{13,1},{2,6},{6,10},{... | collective-permute-start | bytes 1032200 | tf_op jit(solution)/shard_map/ppermute | solution.py:235
  634.1 16.3 %collective-permute-start.11 = (bf16[2,112,768]{2,1,0:T(8,128)(2,1)}, bf16[2,112,768]{2,1,0:T(8,128)(2,1)}, u32[]{:S(2)}, u32[]{:S(2)}) collective-permute-start(bf16[2,112,768]{2,1,0:T(8,128)(2,1)} %get-tuple-element.105), channel_id=1, source_target_pairs={{0,12},{4,0},{8,4},{12,8},{1,13},{5,1},{9,5},{13,9},{2,14},{6,2},{... | collective-permute-start | bytes 1032200 | tf_op jit(solution)/shard_map/ppermute | solution.py:235
  636.3 28.8 %collective-permute-start.10 = (bf16[2,112,768]{2,1,0:T(8,128)(2,1)}, bf16[2,112,768]{2,1,0:T(8,128)(2,1)}, u32[]{:S(2)}, u32[]{:S(2)}) collective-permute-start(bf16[2,112,768]{2,1,0:T(8,128)(2,1)} %get-tuple-element.106), channel_id=1, source_target_pairs={{0,8},{4,12},{8,0},{12,4},{1,9},{5,13},{9,1},{13,5},{2,10},{6,14},... | collective-permute-start | bytes 1032200 | tf_op jit(solution)/shard_map/ppermute | solution.py:235
  643.5 21.7 %copy-start.32 = (f32[2,112,768]{2,1,0:T(8,128)S(1)}, f32[2,112,768]{2,1,0:T(8,128)}, u32[]{:S(2)}) copy-start(f32[2,112,768]{2,1,0:T(8,128)} %copy-done.31) | copy-start | bytes 2064388
  643.5 21.7 %copy-start.76 = (f32[768]{0:T(1024)S(1)}, f32[768]{0:T(1024)}, u32[]{:S(2)}) copy-start(f32[768]{0:T(1024)} %get-tuple-element.116) | copy-start | bytes 9220
  643.5 24.1 %copy-start.79 = (f32[1,768]{1,0:T(1,128)S(1)}, f32[1,768]{1,0:T(1,128)}, u32[]{:S(2)}) copy-start(f32[1,768]{1,0:T(1,128)} %stack.72) | copy-start | bytes 9220
  644.8 22.8 %copy-start.36 = (f32[2,112,768]{2,1,0:T(8,128)S(1)}, f32[2,112,768]{2,1,0:T(8,128)}, u32[]{:S(2)}) copy-start(f32[2,112,768]{2,1,0:T(8,128)} %copy-done.35) | copy-start | bytes 2064388
  668.0 49.2 %collective-permute-start.16 = (bf16[1152]{0:T(1024)(128)(2,1)S(1)}, bf16[1152]{0:T(1024)(128)(2,1)S(1)}, u32[]{:S(2)}, u32[]{:S(2)}) collective-permute-start(bf16[1152]{0:T(1024)(128)(2,1)S(1)} %select_convert_fusion), channel_id=1, source_target_pairs={{0,16},{16,0},{1,17},{17,1},{2,18},{18,2},{3,19},{19,3},{4,20},{20... | collective-permute-start | bytes 6920 | tf_op jit(solution)/shard_map/ppermute | solution.py:17
  668.1 3.9 copy-start.2
  670.5 33.9 %copy-start.75 = (f32[768]{0:T(1024)S(1)}, f32[768]{0:T(1024)}, u32[]{:S(2)}) copy-start(f32[768]{0:T(1024)} %copy-done.74) | copy-start | bytes 9220
  670.5 33.9 %copy-start.78 = (f32[2,112]{1,0:T(2,128)S(1)}, f32[2,112]{1,0:T(2,128)}, u32[]{:S(2)}) copy-start(f32[2,112]{1,0:T(2,128)} %copy-done.77) | copy-start | bytes 2692
  670.5 33.9 %copy-start.80 = (f32[2,112]{1,0:T(2,128)S(1)}, f32[2,112]{1,0:T(2,128)}, u32[]{:S(2)}) copy-start(f32[2,112]{1,0:T(2,128)} %add_rsqrt_fusion.3) | copy-start | bytes 2692
  704.8 10.3 %copy-start.17 = (f32[2,112,768]{2,1,0:T(8,128)S(1)}, f32[2,112,768]{2,1,0:T(8,128)}, u32[]{:S(2)}) copy-start(f32[2,112,768]{2,1,0:T(8,128)} %copy-done.16) | copy-start | bytes 2064388
  713.8 92.5 %collective-permute-start.15 = (bf16[1152,768]{1,0:T(8,128)(2,1)}, bf16[1152,768]{1,0:T(8,128)(2,1)}, u32[]{:S(2)}, u32[]{:S(2)}) collective-permute-start(bf16[1152,768]{1,0:T(8,128)(2,1)} %bitcast_select_fusion), channel_id=1, source_target_pairs={{0,16},{16,0},{1,17},{17,1},{2,18},{18,2},{3,19},{19,3},{4,20},{20... | collective-permute-start | bytes 5308424 | tf_op jit(solution)/shard_map/ppermute | solution.py:17
  716.6 11.0 %collective-permute-start.13 = (f32[6,768]{1,0:T(8,128)S(1)}, f32[6,768]{1,0:T(8,128)S(1)}, u32[]{:S(2)}, u32[]{:S(2)}) collective-permute-start(f32[6,768]{1,0:T(8,128)S(1)} %broadcast_select_fusion.15), channel_id=1, source_target_pairs={{0,16},{16,0},{1,17},{17,1},{2,18},{18,2},{3,19},{19,3},{4,20},{20... | collective-permute-start | bytes 55304 | tf_op jit(solution)/shard_map/ppermute | solution.py:17
  716.7 87.1 %collective-permute-start.12 = (f32[2,112,768]{2,1,0:T(8,128)}, f32[2,112,768]{2,1,0:T(8,128)S(1)}, u32[]{:S(2)}, u32[]{:S(2)}) collective-permute-start(f32[2,112,768]{2,1,0:T(8,128)} %get-tuple-element.84), channel_id=1, source_target_pairs={{0,16},{16,0},{1,17},{17,1},{2,18},{18,2},{3,19},{19,3},{4,20},{20... | collective-permute-start | bytes 2064392 | tf_op jit(solution)/shard_map/ppermute | solution.py:17
  (47 other events, 78.0 us)
Sparse Core Ops, SparseCore 0:
  643.6 68.6 all-reduce.1
